TPU v7x, 256 devices: a whole 4x4x8 slice. The times are simulated.
256 devices in a mesh: band: 64 (over z, x, core), chan: 4 (over y).
Axes of the slice: x: 4, y: 4, z: 8, core: 2. Of those that a mesh axis runs over, the one named last changes fastest.
Arguments:
- mesh_node_state: bfloat16 [8192, 1024], P('band'), may hold values from -6 to 6
- grid_state: bfloat16 [32768, 1024], P('band'), may hold values from -6 to 6
- d_out: bfloat16 [32768, 1024], P('band'), may hold values from -16 to 16
- neighbours: int32 [32768, 4], P('band'), may hold values from 0 to 8191, as said below
- edge_count: int32 [32768], P('band'), may hold values from 1 to 4
- w_proc_qkv: bfloat16 [3, 1024, 1024], P(None, None, 'chan')
- w_proc_out: bfloat16 [1024, 1024], P('chan'), may hold values from -0.1875 to 0.1875
- w_dec_q: bfloat16 [1024, 1024], P(None, 'chan'), may hold values from -0.1875 to 0.1875
- w_dec_kv: bfloat16 [2, 1024, 1024], P(None, None, 'chan'), may hold values from -0.1875 to 0.1875
- w_dec_out: bfloat16 [1024, 1024], P('chan'), may hold values from -0.1875 to 0.1875
Outputs:
- mesh_state_gradient: bfloat16 [8192, 1024], P('band')
- d_grid: bfloat16 [32768, 1024], P('band', 'chan')
- g_proc_qkv: float32 [3, 1024, 1024], P(None, 'band', 'chan')
- g_proc_out: float32 [1024, 1024], P('chan', 'band')
- g_dec_q: float32 [1024, 1024], P('band', 'chan')
- g_dec_kv: float32 [2, 1024, 1024], P(None, 'band', 'chan')
- g_dec_out: float32 [1024, 1024], P('chan', 'band')
Inputs may be any that keep to these rules, and one draw needn't show every extreme that they name: `neighbours`: grid points of rows b*512 to (b+1)*512 - 1 list only mesh nodes of rows b*128 - 8 to (b+1)*128 + 7.
All inputs are finite; a program needn't handle non-finite values.
Results may differ from a plain program's by a relative error of at most 0.03.
Values may be sent and summed in bfloat16 or wider, within the bound.
A program may use at most 128 MiB of HBM per device.

v0:
```python
import jax
import jax.numpy as jnp
from jax import lax
from jax.sharding import PartitionSpec as P

HEAD_DIM = 64
EDGES = 4
WINDOW = 128


EPS = 1e-05
NEG = -1e30


def extended(shard, sides, width):
    for axis, dim in sides:
        peers, length = (lax.axis_size(axis), shard.shape[dim])
        up = [(i, (i + 1) % peers) for i in range(peers - 1)]
        down = [(j, i) for i, j in up]
        last = lax.slice_in_dim(shard, length - width, length, axis=dim)
        leading = lax.slice_in_dim(shard, 0, width, axis=dim)
        before = lax.ppermute(last, axis, up)
        after = lax.ppermute(leading, axis, down)
        shard = jnp.concatenate([before, shard, after], axis=dim)
    return shard


def layer_norm_forward(values):
    values = values.astype(jnp.float32)
    centre = jnp.mean(values, axis=-1, keepdims=True)
    shifted = values - centre
    rstd = lax.rsqrt(jnp.mean(shifted * shifted, axis=-1, keepdims=True) + EPS)
    return (shifted * rstd, rstd)


def layer_norm_backward(normed, rstd, upstream):
    first = jnp.mean(upstream, axis=-1, keepdims=True)
    second = jnp.mean(upstream * normed, axis=-1, keepdims=True)
    return rstd * (upstream - first - normed * second)


def back_dot(left, weight):
    return lax.dot_general(
        left, weight, (((1,), (1,)), ((), ())), preferred_element_type=jnp.float32
    )


def outer_sum(left, right):
    return lax.dot_general(
        left, right, (((0,), (0,)), ((), ())), preferred_element_type=jnp.float32
    )


def window_probs(query_heads, key_heads, base_row, total_rows):
    row_count = query_heads.shape[0]
    scores = jnp.einsum(
        "qhd,khd->hqk", query_heads, key_heads, preferred_element_type=jnp.float32
    ) * HEAD_DIM ** (-0.5)
    query_pos = base_row + jnp.arange(row_count, dtype=jnp.int32)
    key_pos = base_row - row_count + jnp.arange(key_heads.shape[0], dtype=jnp.int32)
    distance = query_pos[:, None] - key_pos[None, :]
    valid_pair = (
        (jnp.abs(distance) <= WINDOW) & (key_pos[None, :] >= 0) & (key_pos[None, :] < total_rows)
    )
    scores = jnp.where(valid_pair[None], scores, NEG)
    return jax.nn.softmax(scores, axis=-1)


def edge_pass(query, keys, values, local, count, upstream):
    row_count = query.shape[0]
    head_count = query.shape[1] // HEAD_DIM
    factor = HEAD_DIM ** (-0.5)
    query_heads = query.astype(jnp.float32).reshape(row_count, head_count, HEAD_DIM)
    keys_at = [
        keys[local[:, j]].astype(jnp.float32).reshape(row_count, head_count, HEAD_DIM)
        for j in range(EDGES)
    ]
    values_at = [
        values[local[:, j]].astype(jnp.float32).reshape(row_count, head_count, HEAD_DIM)
        for j in range(EDGES)
    ]
    scores = jnp.stack([jnp.sum(query_heads * item, axis=-1) for item in keys_at], axis=-1) * factor
    valid_edge = (jnp.arange(EDGES, dtype=jnp.int32)[None, :] < count[:, None])[:, None, :]
    scores = jnp.where(valid_edge, scores, NEG)
    weights = jax.nn.softmax(scores, axis=-1)
    output = weights[..., 0:1] * values_at[0]
    for j in range(1, EDGES):
        output = output + weights[..., j : j + 1] * values_at[j]
    up_heads = upstream.reshape(row_count, head_count, HEAD_DIM)
    dweight = jnp.stack([jnp.sum(up_heads * item, axis=-1) for item in values_at], axis=-1)
    dscore = weights * (dweight - jnp.sum(weights * dweight, axis=-1, keepdims=True))
    dquery = dscore[..., 0:1] * keys_at[0]
    for j in range(1, EDGES):
        dquery = dquery + dscore[..., j : j + 1] * keys_at[j]
    dquery = dquery * factor
    key_terms = jnp.stack(
        [dscore[..., j : j + 1] * query_heads * factor for j in range(EDGES)], axis=0
    )
    value_terms = jnp.stack([weights[..., j : j + 1] * up_heads for j in range(EDGES)], axis=0)
    segment_ids = jnp.transpose(local).reshape(-1)
    dkeys = jax.ops.segment_sum(
        key_terms.reshape(EDGES * row_count, -1), segment_ids, num_segments=keys.shape[0]
    )
    dvalues = jax.ops.segment_sum(
        value_terms.reshape(EDGES * row_count, -1), segment_ids, num_segments=keys.shape[0]
    )
    return (output.reshape(row_count, -1), dquery.reshape(row_count, -1), dkeys, dvalues)


def body(
    mesh_node_state,
    grid_state,
    d_out,
    neighbours,
    edge_count,
    w_proc_qkv,
    w_proc_out,
    w_dec_q,
    w_dec_kv,
    w_dec_out,
):
    brain_float_sixteen = jnp.bfloat16
    band_count = lax.axis_size("band")
    band_index = lax.axis_index("band")
    mesh_rows = mesh_node_state.shape[0]
    total_rows = mesh_rows * band_count
    base_row = band_index * mesh_rows
    local_width = w_proc_qkv.shape[2]
    head_count = local_width // HEAD_DIM
    factor = HEAD_DIM ** (-0.5)
    input_centred_scaled, inverse_deviation_input = layer_norm_forward(mesh_node_state)
    mesh_state_normalised = input_centred_scaled.astype(brain_float_sixteen)
    query_p = jnp.dot(
        mesh_state_normalised, w_proc_qkv[0], preferred_element_type=jnp.float32
    ).astype(brain_float_sixteen)
    key_p = jnp.dot(
        mesh_state_normalised, w_proc_qkv[1], preferred_element_type=jnp.float32
    ).astype(brain_float_sixteen)
    value_p = jnp.dot(
        mesh_state_normalised, w_proc_qkv[2], preferred_element_type=jnp.float32
    ).astype(brain_float_sixteen)
    window_kv = extended(jnp.stack([key_p, value_p]), (("band", 1),), mesh_rows)
    query_heads = query_p.reshape(mesh_rows, head_count, HEAD_DIM)
    key_heads = window_kv[0].reshape(3 * mesh_rows, head_count, HEAD_DIM)
    value_heads = window_kv[1].reshape(3 * mesh_rows, head_count, HEAD_DIM)
    probs = window_probs(query_heads, key_heads, base_row, total_rows)
    probs_b = probs.astype(brain_float_sixteen)
    attended = jnp.einsum("hqk,khd->qhd", probs_b, value_heads, preferred_element_type=jnp.float32)
    attended = attended.reshape(mesh_rows, local_width).astype(brain_float_sixteen)
    mixed = lax.psum(
        jnp.dot(attended, w_proc_out, preferred_element_type=jnp.float32).astype(jnp.bfloat16),
        "chan",
    ).astype(jnp.float32)
    state_out = (mesh_node_state.astype(jnp.float32) + mixed).astype(brain_float_sixteen)
    yhat, rstd_y = layer_norm_forward(state_out)
    state_normed = yhat.astype(brain_float_sixteen)
    key_d = jnp.dot(state_normed, w_dec_kv[0], preferred_element_type=jnp.float32).astype(
        brain_float_sixteen
    )
    value_d = jnp.dot(state_normed, w_dec_kv[1], preferred_element_type=jnp.float32).astype(
        brain_float_sixteen
    )
    decoder_kv = extended(jnp.stack([key_d, value_d]), (("band", 1),), mesh_rows)
    ghat, rstd_g = layer_norm_forward(grid_state)
    grid_normed = ghat.astype(brain_float_sixteen)
    query_d = jnp.dot(grid_normed, w_dec_q, preferred_element_type=jnp.float32).astype(
        brain_float_sixteen
    )
    upstream = back_dot(d_out, w_dec_out)
    local = neighbours - base_row + mesh_rows
    dec_out, dquery, dkey_ext_d, dvalue_ext_d = edge_pass(
        query_d, decoder_kv[0], decoder_kv[1], local, edge_count, upstream
    )
    dkv_dec_ext = jnp.stack([dkey_ext_d, dvalue_ext_d])
    dec_rims = jnp.concatenate(
        [dkv_dec_ext[:, :mesh_rows], dkv_dec_ext[:, mesh_rows + mesh_rows :]], axis=1
    )
    dec_returned = extended(dec_rims.astype(jnp.bfloat16), (("band", 1),), mesh_rows).astype(
        dec_rims.dtype
    )
    dkv_dec = dkv_dec_ext[:, mesh_rows : mesh_rows + mesh_rows]
    dkv_dec = dkv_dec.at[:, :mesh_rows].add(dec_returned[:, :mesh_rows])
    dkv_dec = dkv_dec.at[:, mesh_rows - mesh_rows :].add(dec_returned[:, 3 * mesh_rows :])
    dkv_dec = dkv_dec.astype(brain_float_sixteen)
    dec_out = dec_out.astype(brain_float_sixteen)
    dquery = dquery.astype(brain_float_sixteen)
    dkey_d = dkv_dec[0]
    dvalue_d = dkv_dec[1]
    grad_dec_out = outer_sum(dec_out, d_out)
    grad_dec_q = outer_sum(grid_normed, dquery)
    grad_dec_kv = jnp.stack([outer_sum(state_normed, dkey_d), outer_sum(state_normed, dvalue_d)])
    grid_part = back_dot(dquery, w_dec_q)
    state_part = back_dot(dkey_d, w_dec_kv[0]) + back_dot(dvalue_d, w_dec_kv[1])
    feature_count = grid_state.shape[1]
    share_width = feature_count // lax.axis_size("chan")
    share_start = lax.axis_index("chan") * share_width
    grid_total, state_total = (
        lax.psum(grid_part.astype(jnp.bfloat16), "chan").astype(jnp.float32),
        lax.psum(state_part.astype(jnp.bfloat16), "chan").astype(jnp.float32),
    )
    grid_grad = d_out.astype(jnp.float32) + layer_norm_backward(ghat, rstd_g, grid_total)
    d_grid = lax.dynamic_slice_in_dim(grid_grad, share_start, share_width, 1).astype(
        brain_float_sixteen
    )
    state_gradient_value = layer_norm_backward(yhat, rstd_y, state_total)
    state_grad_b = state_gradient_value.astype(brain_float_sixteen)
    grad_proc_out = outer_sum(attended, state_grad_b)
    dattended = back_dot(state_grad_b, w_proc_out).astype(brain_float_sixteen)
    grad_heads = dattended.reshape(mesh_rows, head_count, HEAD_DIM)
    dvalue_ext = jnp.einsum("hqk,qhd->khd", probs_b, grad_heads, preferred_element_type=jnp.float32)
    dprob = jnp.einsum("qhd,khd->hqk", grad_heads, value_heads, preferred_element_type=jnp.float32)
    centre = jnp.sum(probs * dprob, axis=-1, keepdims=True)
    dscore = (probs * (dprob - centre)).astype(brain_float_sixteen)
    dquery_p = (
        jnp.einsum("hqk,khd->qhd", dscore, key_heads, preferred_element_type=jnp.float32) * factor
    )
    dkey_ext = (
        jnp.einsum("hqk,qhd->khd", dscore, query_heads, preferred_element_type=jnp.float32) * factor
    )
    dkv_ext = jnp.stack([dkey_ext, dvalue_ext]).reshape(2, 3 * mesh_rows, local_width)
    rims = jnp.concatenate([dkv_ext[:, :mesh_rows], dkv_ext[:, 2 * mesh_rows :]], axis=1)
    returned = extended(rims.astype(jnp.bfloat16), (("band", 1),), mesh_rows).astype(rims.dtype)
    dkv_own = (
        dkv_ext[:, mesh_rows : 2 * mesh_rows]
        + returned[:, :mesh_rows]
        + returned[:, 3 * mesh_rows :]
    )
    dkv_own = dkv_own.astype(brain_float_sixteen)
    dquery_p = dquery_p.reshape(mesh_rows, local_width).astype(brain_float_sixteen)
    dkey_p = dkv_own[0]
    dvalue_p = dkv_own[1]
    mesh_part = (
        back_dot(dquery_p, w_proc_qkv[0])
        + back_dot(dkey_p, w_proc_qkv[1])
        + back_dot(dvalue_p, w_proc_qkv[2])
    )
    mesh_gradient_total = lax.psum(mesh_part.astype(jnp.bfloat16), "chan").astype(jnp.float32)
    mesh_state_gradient = (
        state_gradient_value
        + layer_norm_backward(input_centred_scaled, inverse_deviation_input, mesh_gradient_total)
    ).astype(brain_float_sixteen)
    grad_proc_qkv = jnp.stack(
        [
            outer_sum(mesh_state_normalised, dquery_p),
            outer_sum(mesh_state_normalised, dkey_p),
            outer_sum(mesh_state_normalised, dvalue_p),
        ]
    )
    summed = (
        lax.psum_scatter(grad_proc_qkv, "band", scatter_dimension=1, tiled=True),
        lax.psum_scatter(grad_proc_out, "band", scatter_dimension=1, tiled=True),
        lax.psum_scatter(grad_dec_q, "band", scatter_dimension=0, tiled=True),
        lax.psum_scatter(grad_dec_kv, "band", scatter_dimension=1, tiled=True),
        lax.psum_scatter(grad_dec_out, "band", scatter_dimension=1, tiled=True),
    )
    return (mesh_state_gradient, d_grid, summed[0], summed[1], summed[2], summed[3], summed[4])


def solution(mesh):
    placed = (
        P("band", None),
        P("band", None),
        P("band", None),
        P("band", None),
        P("band"),
        P(None, None, "chan"),
        P("chan", None),
        P(None, "chan"),
        P(None, None, "chan"),
        P("chan", None),
    )
    return jax.shard_map(
        body,
        mesh=mesh,
        in_specs=placed,
        out_specs=(
            P("band", None),
            P("band", "chan"),
            P(None, "band", "chan"),
            P("chan", "band"),
            P("band", "chan"),
            P(None, "band", "chan"),
            P("chan", "band"),
        ),
        check_vma=False,
    )
```

profile of v0, /device:TPU:1, one launch (start us, length us, event | category | flops | bytes accessed | tf_op | source)
XLA Modules:
  0.0 1029.7 jit_solution(10825200113526318181)
XLA Ops:
  12.5 5.1 collective-permute-start.1
  26.0 49.8 %all-reduce.5.cloned.1.call-done = bf16[128,1024]{1,0:T(8,128)(2,1)} async-done(((bf16[128,1024]{1,0:T(8,128)(2,1)}), bf16[128,1024]{1,0:T(8,128)(2,1)}) %all-reduce.5.cloned.1.call-update) | async-done | bytes 262160 | tf_op jit(solution)/shard_map/psum | solution.py:150
  79.9 4.7 collective-permute-start.3
  84.6 3.0 collective-permute-start.2
  89.6 2.6 gather_fusion.3
  92.2 2.6 gather_fusion.7
  101.8 2.6 gather_fusion.4
  120.3 2.9 bitcast_reduce_fusion.7
  130.4 3.0 copy.92
  135.2 4.8 copy.94
  140.0 5.3 reshape.486
  145.2 12.3 %scatter_custom_fusion.1 = f32[384,256]{1,0:T(8,128)S(1)} fusion(s32[2048]{0:T(1024)S(1)} %bitcast.230, f32[2048,256]{1,0:T(8,128)} %copy.92, f32[]{:T(128)} %constant.110.clone.1), kind=kCustom, calls=%fused_computation.180 | custom fusion | flops 524288 | bytes 393728 | tf_op jit(solution)/shard_map/scatter-add | solution.py:104
  157.5 12.1 %scatter_custom_fusion = f32[384,256]{1,0:T(8,128)S(1)} fusion(s32[2048]{0:T(1024)S(1)} %bitcast.231, f32[2048,256]{1,0:T(8,128)} %reshape.486, f32[]{:T(128)} %constant.110.clone.1), kind=kCustom, calls=%fused_computation.182 | custom fusion | flops 524288 | bytes 393728 | tf_op jit(solution)/shard_map/scatter-add | solution.py:101
  169.7 4.5 collective-permute-start.4
  183.5 48.8 %all-reduce.7.cloned.1.call-done = bf16[128,1024]{1,0:T(8,128)(2,1)} async-done(((bf16[128,1024]{1,0:T(8,128)(2,1)}), bf16[128,1024]{1,0:T(8,128)(2,1)}) %all-reduce.7.cloned.1.call-update) | async-done | bytes 262160 | tf_op jit(solution)/shard_map/psum | solution.py:199
  240.7 5.8 collective-permute-start.6
  248.8 4.0 collective-permute-done.7
  257.6 2.6 fusion.61
  269.0 39.4 %all-reduce.9.cloned.1.call-done = (bf16[128,1024]{1,0:T(8,128)(2,1)}, bf16[512,1024]{1,0:T(8,128)(2,1)}) async-done(((bf16[128,1024]{1,0:T(8,128)(2,1)}, bf16[512,1024]{1,0:T(8,128)(2,1)}), (bf16[128,1024]{1,0:T(8,128)(2,1)}, bf16[512,1024]{1,0:T(8,128)(2,1)})) %all-reduce.9.cloned.1.call-update) | async-done | bytes 1310736 | tf_op jit(solution)/shard_map/psum | solution.py:237
  313.5 135.5 %reduce-scatter.14.cloned.1.call-done = f32[256,16]{0,1:T(8,128)} async-done(((f32[256,1024]{0,1:T(8,128)}), f32[256,16]{0,1:T(8,128)}) %reduce-scatter.14.cloned.1.call-update) | async-done | bytes 16400 | tf_op jit(solution)/shard_map/reduce_scatter | solution.py:254
  449.0 142.1 %reduce-scatter.10.cloned.1.call-done = f32[16,256]{1,0:T(8,128)} async-done(((f32[1024,256]{1,0:T(8,128)}), f32[16,256]{1,0:T(8,128)}) %reduce-scatter.10.cloned.1.call-update) | async-done | bytes 16400 | tf_op jit(solution)/shard_map/reduce_scatter | solution.py:252
  591.1 142.2 %reduce-scatter.8.cloned.1.call-done = f32[256,16]{0,1:T(8,128)} async-done(((f32[256,1024]{0,1:T(8,128)}), f32[256,16]{0,1:T(8,128)}) %reduce-scatter.8.cloned.1.call-update) | async-done | bytes 16400 | tf_op jit(solution)/shard_map/reduce_scatter | solution.py:251
  733.3 143.9 %reduce-scatter.12.cloned.1.call-done = f32[2,16,256]{2,1,0:T(8,128)} async-done(((f32[2,1024,256]{2,1,0:T(8,128)}), f32[2,16,256]{2,1,0:T(8,128)}) %reduce-scatter.12.cloned.1.call-update) | async-done | bytes 32784 | tf_op jit(solution)/shard_map/reduce_scatter | solution.py:253
  877.2 145.7 %reduce-scatter.6.cloned.1.call-done = f32[3,16,256]{2,1,0:T(8,128)} async-done(((f32[3,1024,256]{2,1,0:T(8,128)}), f32[3,16,256]{2,1,0:T(8,128)}) %reduce-scatter.6.cloned.1.call-update) | async-done | bytes 49168 | tf_op jit(solution)/shard_map/reduce_scatter | solution.py:250
  (250 shorter events, 89.1 us)
Async XLA Ops:
  7.2 113.1 %copy-start = (bf16[1024,256]{1,0:T(8,128)(2,1)S(1)}, bf16[1024,256]{1,0:T(8,128)(2,1)}, u32[]{:S(2)}) copy-start(bf16[1024,256]{1,0:T(8,128)(2,1)} %param.25) | copy-start | bytes 1572868
  7.2 68.6 %all-reduce.5.cloned.1.call-start = ((), (), s32[]{:S(2)}) async-start(), calls=%async_computation.5 | async-start | bytes 524288 | tf_op jit(solution)/shard_map/psum | solution.py:150
  8.4 12.8 %copy-start.35 = (f32[128]{0:T(128)}, f32[128]{0:T(128)S(1)}, u32[]{:S(2)}) copy-start(f32[128]{0:T(128)S(1)} %broadcast_multiply_fusion.12) | copy-start | bytes 1540
  12.5 9.5 collective-permute-start.1
  17.7 4.4 collective-permute-start
  21.3 99.0 %copy-start.40 = (f32[512]{0:T(512)}, f32[512]{0:T(512)S(1)}, u32[]{:S(2)}) copy-start(f32[512]{0:T(512)S(1)} %broadcast_multiply_fusion.6) | copy-start | bytes 6148
  21.9 98.3 %copy-start.42 = (f32[512]{0:T(512)}, f32[512]{0:T(512)S(1)}, u32[]{:S(2)}) copy-start(f32[512]{0:T(512)S(1)} %add_rsqrt_fusion) | copy-start | bytes 6148
  24.5 55.3 %copy-start.28 = (bf16[4,64,128]{2,1,0:T(8,128)(2,1)}, bf16[4,64,128]{2,1,0:T(8,128)(2,1)S(1)}, u32[]{:S(2)}) copy-start(bf16[4,64,128]{2,1,0:T(8,128)(2,1)S(1)} %convolution_convert_fusion.6) | copy-start | bytes 196612
  25.9 206.4 %all-reduce.7.cloned.1.call-start = ((), (), s32[]{:S(2)}) async-start(), calls=%async_computation.6 | async-start | bytes 524288 | tf_op jit(solution)/shard_map/psum | solution.py:199
  79.9 8.4 collective-permute-start.3
  84.6 4.9 collective-permute-start.2
  169.7 8.5 collective-permute-start.4
  174.2 6.3 collective-permute-start.5
  180.6 51.8 %copy-start.38 = (f32[128]{0:T(128)S(1)}, f32[128]{0:T(128)}, u32[]{:S(2)}) copy-start(f32[128]{0:T(128)} %copy-done.37) | copy-start | bytes 1540
  180.6 51.8 %copy-start.47 = (f32[128]{0:T(128)S(1)}, f32[128]{0:T(128)}, u32[]{:S(2)}) copy-start(f32[128]{0:T(128)} %copy-done.46) | copy-start | bytes 1540
  181.9 54.4 %copy-start.26 = (bf16[128,256]{0,1:T(8,128)(2,1)S(1)}, bf16[128,256]{0,1:T(8,128)(2,1)}, u32[]{:S(2)}) copy-start(bf16[128,256]{0,1:T(8,128)(2,1)} %copy-done.25) | copy-start | bytes 196612
  181.9 126.5 %all-reduce.9.cloned.1.call-start = ((), (), s32[]{:S(2)}) async-start(), calls=%async_computation.12 | async-start | bytes 2621440 | tf_op jit(solution)/shard_map/psum | solution.py:237
  240.7 8.0 collective-permute-start.6
  246.5 6.3 collective-permute-start.7
  254.5 194.5 %reduce-scatter.14.cloned.1.call-start = ((), (), s32[]{:S(2)}) async-start(), calls=%async_computation.11 | async-start | bytes 1064960 | tf_op jit(solution)/shard_map/reduce_scatter | solution.py:254
  257.6 333.5 %reduce-scatter.10.cloned.1.call-start = ((), (), s32[]{:S(2)}) async-start(), calls=%async_computation.9 | async-start | bytes 1064960 | tf_op jit(solution)/shard_map/reduce_scatter | solution.py:252
  260.3 473.0 %reduce-scatter.8.cloned.1.call-start = ((), (), s32[]{:S(2)}) async-start(), calls=%async_computation.8 | async-start | bytes 1064960 | tf_op jit(solution)/shard_map/reduce_scatter | solution.py:251
  262.6 614.6 %reduce-scatter.12.cloned.1.call-start = ((), (), s32[]{:S(2)}) async-start(), calls=%async_computation.10 | async-start | bytes 2129920 | tf_op jit(solution)/shard_map/reduce_scatter | solution.py:253
  265.0 757.8 %reduce-scatter.6.cloned.1.call-start = ((), (), s32[]{:S(2)}) async-start(), calls=%async_computation.7 | async-start | bytes 3194880 | tf_op jit(solution)/shard_map/reduce_scatter | solution.py:250
  (49 other events, 186.2 us)
Sparse Core Ops, SparseCore 0:
  26.0 49.7 all-reduce.4
  182.0 50.2 all-reduce.6
  254.7 53.7 all-reduce.8
  312.9 136.0 reduce-scatter.13
  453.4 137.6 reduce-scatter.9
  595.5 137.6 reduce-scatter.7
  737.9 139.2 reduce-scatter.11
  882.4 140.3 reduce-scatter.5
where the time goes:
time: 1040 us; the launch traced here: 1030 us
  waiting for transfers between devices  856 us (82%)
  other arithmetic  49.5 us (5%)
  local copies, waits for them, and re-layouts  49.4 us (5%)
  matrix products  30.2 us (3%)
  starting transfers between devices  29.5 us (3%)
  between operations  15.4 us (1%)
    reduce_scatter x1, waiting for transfers between devices, body(): lax.psum_scatter(grad_proc_qkv, 'band', scatter_dimension=1, tiled=True)  146 us
    reduce_scatter x1, waiting for transfers between devices, body(): lax.psum_scatter(grad_dec_kv, 'band', scatter_dimension=1, tiled=True)  144 us
    reduce_scatter x1, waiting for transfers between devices, body(): lax.psum_scatter(grad_proc_out, 'band', scatter_dimension=1, tiled=True)  142 us
    reduce_scatter x1, waiting for transfers between devices, body(): lax.psum_scatter(grad_dec_q, 'band', scatter_dimension=0, tiled=True)  142 us
    reduce_scatter x1, waiting for transfers between devices, body(): lax.psum_scatter(grad_dec_out, 'band', scatter_dimension=1, tiled=True)  136 us
    psum x1, waiting for transfers between devices, body(): lax.psum(jnp.dot(attended, w_proc_out, preferred_element_type=jnp.float32...  49.8 us
    psum x1, waiting for transfers between devices, body(): lax.psum(state_part.astype(jnp.bfloat16), 'chan').astype(jnp.float32)  48.8 us
    psum x1, waiting for transfers between devices, body(): lax.psum(mesh_part.astype(jnp.bfloat16), 'chan').astype(jnp.float32)  39.4 us
  transfers between devices with their start and end apart: 16, of which 12 were waited for; matrix products, arithmetic and copies ran while one was open for 2% of the time, Pallas kernels for 0%

commit v1 on v0

--- a/solution.py
+++ b/solution.py
@@ -1,6 +1,8 @@
 import jax
 import jax.numpy as jnp
 from jax import lax
+from jax.experimental import pallas as pl
+from jax.experimental.pallas import tpu as pltpu
 from jax.sharding import PartitionSpec as P
 
 HEAD_DIM = 64
@@ -8,6 +10,7 @@
 WINDOW = 128
 
 
+NZ, NX, NC = 8, 4, 2
 EPS = 1e-05
 NEG = -1e30
 
@@ -105,6 +108,94 @@
         value_terms.reshape(EDGES * row_count, -1), segment_ids, num_segments=keys.shape[0]
     )
     return (output.reshape(row_count, -1), dquery.reshape(row_count, -1), dkeys, dvalues)
+
+
+def band_reduce_kernel(g_hbm, out_ref, g, ra, hb, rb, hc, rc, in_sem, send, recv):
+    band = lax.axis_index("band")
+    core = lax.rem(band, NC)
+    x = lax.rem(lax.div(band, NC), NX)
+    z = lax.div(band, NC * NX)
+    load = pltpu.make_async_copy(g_hbm, g, in_sem)
+    load.start()
+
+    def at(zz, xx, cc):
+        return {"band": (zz * NX + xx) * NC + cc}
+
+    pair = at(z, x, 1 - core)
+    x_peers = [at(z, lax.rem(x + d, NX), core) for d in range(1, NX)]
+    z_peers = [at(lax.rem(z + d, NZ), x, core) for d in range(1, NZ)]
+    barrier = pltpu.get_barrier_semaphore()
+    for peer in [pair] + x_peers + z_peers:
+        pl.semaphore_signal(barrier, inc=1, device_id=peer, device_id_type=pl.DeviceIdType.MESH)
+    pl.semaphore_wait(barrier, 1 + (NX - 1) + (NZ - 1))
+    load.wait()
+
+    def push(src, dst, slot, peer):
+        copy = pltpu.make_async_remote_copy(
+            src_ref=src, dst_ref=dst, send_sem=send.at[slot], recv_sem=recv.at[slot],
+            device_id=peer, device_id_type=pl.DeviceIdType.MESH,
+        )
+        copy.start()
+        return copy
+
+    first = push(g.at[1 - core], ra, 0, pair)
+    first.wait()
+
+    def add_pair(i, carry):
+        xx, zz = lax.div(i, NZ), lax.rem(i, NZ)
+        hb[xx, zz] = (g[core, xx, zz].astype(jnp.float32) + ra[xx, zz].astype(jnp.float32)).astype(jnp.bfloat16)
+        return carry
+
+    lax.fori_loop(0, NX * NZ, add_pair, 0)
+    copies = [push(hb.at[lax.rem(x + d, NX)], rb.at[d - 1], d, x_peers[d - 1]) for d in range(1, NX)]
+    for copy in copies:
+        copy.wait()
+
+    def add_x(zz, carry):
+        total = hb[x, zz].astype(jnp.float32)
+        for d in range(NX - 1):
+            total = total + rb[d, zz].astype(jnp.float32)
+        hc[zz] = total.astype(jnp.bfloat16)
+        return carry
+
+    lax.fori_loop(0, NZ, add_x, 0)
+    copies = [push(hc.at[lax.rem(z + d, NZ)], rc.at[d - 1], NX - 1 + d, z_peers[d - 1]) for d in range(1, NZ)]
+    for copy in copies:
+        copy.wait()
+    total = hc[z].astype(jnp.float32)
+    for d in range(NZ - 1):
+        total = total + rc[d].astype(jnp.float32)
+    out_ref[...] = total
+
+
+def band_reduce(grads):
+    count, rows, columns = grads.shape
+    part = rows // (NZ * NX * NC)
+    grads = grads.astype(jnp.bfloat16).reshape(count, NZ, NX, NC, part, columns)
+    grads = jnp.transpose(grads, (3, 2, 1, 0, 4, 5)).reshape(NC, NX, NZ, count * part, columns)
+    chunk = (count * part, columns)
+    slots = 1 + (NX - 1) + (NZ - 1)
+    out = pl.pallas_call(
+        band_reduce_kernel,
+        out_shape=jax.ShapeDtypeStruct(chunk, jnp.float32),
+        in_specs=[pl.BlockSpec(memory_space=pl.ANY)],
+        out_specs=pl.BlockSpec(memory_space=pltpu.VMEM),
+        scratch_shapes=[
+            pltpu.VMEM((NC, NX, NZ) + chunk, jnp.bfloat16),
+            pltpu.VMEM((NX, NZ) + chunk, jnp.bfloat16),
+            pltpu.VMEM((NX, NZ) + chunk, jnp.bfloat16),
+            pltpu.VMEM((NX - 1, NZ) + chunk, jnp.bfloat16),
+            pltpu.VMEM((NZ,) + chunk, jnp.bfloat16),
+            pltpu.VMEM((NZ - 1,) + chunk, jnp.bfloat16),
+            pltpu.SemaphoreType.DMA,
+            pltpu.SemaphoreType.DMA((slots,)),
+            pltpu.SemaphoreType.DMA((slots,)),
+        ],
+        compiler_params=pltpu.CompilerParams(
+            collective_id=0, has_side_effects=True, vmem_limit_bytes=40 * 2**20
+        ),
+    )(grads)
+    return out.reshape(count, part, columns)
 
 
 def body(
@@ -186,7 +277,7 @@
     dquery = dquery.astype(brain_float_sixteen)
     dkey_d = dkv_dec[0]
     dvalue_d = dkv_dec[1]
-    grad_dec_out = outer_sum(dec_out, d_out)
+    grad_dec_out = outer_sum(d_out, dec_out)
     grad_dec_q = outer_sum(grid_normed, dquery)
     grad_dec_kv = jnp.stack([outer_sum(state_normed, dkey_d), outer_sum(state_normed, dvalue_d)])
     grid_part = back_dot(dquery, w_dec_q)
@@ -204,7 +295,7 @@
     )
     state_gradient_value = layer_norm_backward(yhat, rstd_y, state_total)
     state_grad_b = state_gradient_value.astype(brain_float_sixteen)
-    grad_proc_out = outer_sum(attended, state_grad_b)
+    grad_proc_out = outer_sum(state_grad_b, attended)
     dattended = back_dot(state_grad_b, w_proc_out).astype(brain_float_sixteen)
     grad_heads = dattended.reshape(mesh_rows, head_count, HEAD_DIM)
     dvalue_ext = jnp.einsum("hqk,qhd->khd", probs_b, grad_heads, preferred_element_type=jnp.float32)
@@ -246,14 +337,12 @@
             outer_sum(mesh_state_normalised, dvalue_p),
         ]
     )
-    summed = (
-        lax.psum_scatter(grad_proc_qkv, "band", scatter_dimension=1, tiled=True),
-        lax.psum_scatter(grad_proc_out, "band", scatter_dimension=1, tiled=True),
-        lax.psum_scatter(grad_dec_q, "band", scatter_dimension=0, tiled=True),
-        lax.psum_scatter(grad_dec_kv, "band", scatter_dimension=1, tiled=True),
-        lax.psum_scatter(grad_dec_out, "band", scatter_dimension=1, tiled=True),
-    )
-    return (mesh_state_gradient, d_grid, summed[0], summed[1], summed[2], summed[3], summed[4])
+    summed = band_reduce(
+        jnp.concatenate(
+            [grad_proc_qkv, grad_proc_out[None], grad_dec_q[None], grad_dec_kv, grad_dec_out[None]]
+        )
+    )
+    return (mesh_state_gradient, d_grid, summed[0:3], summed[3].T, summed[4], summed[5:7], summed[7].T)
 
 
 def solution(mesh):

time: 1040 us -> 402 us (0.39)
  waiting for transfers between devices: 856 us -> 143 us
  Pallas kernels: 0 us -> 51.9 us
  local copies, waits for them, and re-layouts: 49.4 us -> 72.2 us
    reduce_scatter x5 -> x0, waiting for transfers between devices: 709 us -> none  [the longest x1 146 us: body(): lax.psum_scatter(grad_proc_qkv, 'band', scatter_dimension=1, tiled=True)]
    pallas_call x0 -> x1, Pallas kernels: none -> 51.9 us  [band_reduce(): pl.pallas_call(band_reduce_kernel, out_shape=jax.ShapeDtypeStruct(chunk,...]
    mul x1 -> x9, local copies, waits for them, and re-layouts: 0.01 us -> 13.1 us  [edge_pass(): dscore[..., j:j + 1] * query_heads * factor]
  transfers between devices with their start and end apart: 16 -> 11, of which waited for: 12 -> 6; matrix products, arithmetic and copies ran while one was open for 2% -> 8% of each run, Pallas kernels for 0% -> 0%
where the time goes in v1:
time: 402 us; the launch traced here: 400 us
  waiting for transfers between devices  143 us (36%)
  local copies, waits for them, and re-layouts  72.2 us (18%)
  other arithmetic  55.5 us (14%)
  Pallas kernels  51.9 us (13%)
  matrix products  33.4 us (8%)
  starting transfers between devices  29.1 us (7%)
  between operations  15.2 us (4%)
    pallas_call x1, Pallas kernels, band_reduce(): pl.pallas_call(band_reduce_kernel, out_shape=jax.ShapeDtypeStruct(chunk,...  51.9 us
    psum x1, waiting for transfers between devices, body(): lax.psum(jnp.dot(attended, w_proc_out, preferred_element_type=jnp.float32...  49.8 us
    psum x1, waiting for transfers between devices, body(): lax.psum(state_part.astype(jnp.bfloat16), 'chan').astype(jnp.float32)  46.3 us
    psum x1, waiting for transfers between devices, body(): lax.psum(mesh_part.astype(jnp.bfloat16), 'chan').astype(jnp.float32)  42.9 us
    ppermute x4, starting transfers between devices, extended(): before = lax.ppermute(last, axis, up)  15 us
    gather x8, local copies, waits for them, and re-layouts, edge_pass(): values[local[:, j]].astype(jnp.float32)  15 us
    ppermute x4, starting transfers between devices, extended(): after = lax.ppermute(leading, axis, down)  14 us
    mul x9, local copies, waits for them, and re-layouts, edge_pass(): dscore[..., j:j + 1] * query_heads * factor  13.1 us
  transfers between devices with their start and end apart: 11, of which 6 were waited for; matrix products, arithmetic and copies ran while one was open for 8% of the time, Pallas kernels for 0%

profile of v1, /device:TPU:1, one launch (start us, length us, event | category | flops | bytes accessed | tf_op | source)
XLA Modules:
  0.0 400.4 jit_solution(15541773611569911712)
XLA Ops:
  12.5 5.2 %collective-permute-start.1 = (bf16[2,128,256]{2,1,0:T(8,128)(2,1)S(1)}, bf16[2,128,256]{2,1,0:T(8,128)(2,1)S(1)}, u32[]{:S(2)}, u32[]{:S(2)}) collective-permute-start(bf16[2,128,256]{2,1,0:T(8,128)(2,1)S(1)} %pad_maximum_fusion.12), channel_id=1, source_target_pairs={{4,0},{8,4},{12,8},{16,12},{20,16},{24,20},{28,24},{32,28},{36,32}... | collective-permute-start | bytes 393224 | tf_op jit(solution)/shard_map/ppermute | solution.py:26
  26.0 49.8 %all-reduce.5.cloned.1.call-done = bf16[128,1024]{1,0:T(8,128)(2,1)} async-done(((bf16[128,1024]{1,0:T(8,128)(2,1)}), bf16[128,1024]{1,0:T(8,128)(2,1)}) %all-reduce.5.cloned.1.call-update) | async-done | bytes 262160 | tf_op jit(solution)/shard_map/psum | solution.py:241
  79.8 4.7 %collective-permute-start.3 = (bf16[2,128,256]{2,1,0:T(8,128)(2,1)S(1)}, bf16[2,128,256]{2,1,0:T(8,128)(2,1)S(1)}, u32[]{:S(2)}, u32[]{:S(2)}) collective-permute-start(bf16[2,128,256]{2,1,0:T(8,128)(2,1)S(1)} %pad_maximum_fusion.13), channel_id=1, source_target_pairs={{4,0},{8,4},{12,8},{16,12},{20,16},{24,20},{28,24},{32,28},{36,32}... | collective-permute-start | bytes 393224 | tf_op jit(solution)/shard_map/ppermute | solution.py:26
  84.6 3.0 collective-permute-start.2
  93.5 2.6 gather_fusion.2
  96.1 2.6 gather_fusion.6
  100.6 2.6 gather_fusion.4
  103.2 2.6 gather_fusion.1
  105.8 2.6 gather_fusion.5
  117.8 2.9 multiply_reduce_fusion.5
  127.9 2.9 copy.106
  133.7 4.8 %copy.130 = f32[4,512,4,64]{3,2,1,0:T(4,128)} copy(f32[4,512,4,64]{1,3,2,0:T(8,128)} %pad_maximum_fusion) | data formatting | bytes 4194304 | tf_op jit(solution)/shard_map/reshape | solution.py:105
  138.5 5.3 %reshape.602 = f32[2048,256]{1,0:T(8,128)} reshape(f32[4,512,4,64]{3,2,1,0:T(4,128)} %copy.130) | data formatting | bytes 4194304 | tf_op jit(solution)/shard_map/reshape | solution.py:105
  143.8 12.3 %scatter_custom_fusion.1 = f32[384,256]{1,0:T(8,128)S(1)} fusion(s32[2048]{0:T(1024)} %bitcast.323, f32[2048,256]{1,0:T(8,128)} %copy.106, f32[]{:T(128)} %constant.110.clone.1), kind=kCustom, calls=%fused_computation.185 | custom fusion | flops 524288 | bytes 393728 | tf_op jit(solution)/shard_map/scatter-add | solution.py:107
  156.1 12.7 %scatter_custom_fusion = f32[384,256]{1,0:T(8,128)} fusion(s32[2048]{0:T(1024)} %bitcast.324, f32[2048,256]{1,0:T(8,128)} %reshape.602, f32[]{:T(128)} %constant.110.clone.1), kind=kCustom, calls=%fused_computation.187 | custom fusion | flops 524288 | bytes 393728 | tf_op jit(solution)/shard_map/scatter-add | solution.py:104
  170.6 4.3 %collective-permute-start.4 = (bf16[2,128,256]{2,1,0:T(8,128)(2,1)}, bf16[2,128,256]{2,1,0:T(8,128)(2,1)}, u32[]{:S(2)}, u32[]{:S(2)}) collective-permute-start(bf16[2,128,256]{2,1,0:T(8,128)(2,1)} %get-tuple-element.79), channel_id=1, source_target_pairs={{0,4},{4,8},{8,12},{12,16},{16,20},{20,24},{24,28},{28,32},{32,36}... | collective-permute-start | bytes 393224 | tf_op jit(solution)/shard_map/ppermute | solution.py:25
  193.7 3.3 convolution_convert_fusion
  196.9 46.3 %all-reduce.7.cloned.1.call-done = bf16[128,1024]{1,0:T(8,128)(2,1)} async-done(((bf16[128,1024]{1,0:T(8,128)(2,1)}), bf16[128,1024]{1,0:T(8,128)(2,1)}) %all-reduce.7.cloned.1.call-update) | async-done | bytes 262160 | tf_op jit(solution)/shard_map/psum | solution.py:290
  259.0 5.8 %collective-permute-start.6 = (bf16[2,128,256]{2,1,0:T(8,128)(2,1)S(1)}, bf16[2,128,256]{2,1,0:T(8,128)(2,1)S(1)}, u32[]{:S(2)}, u32[]{:S(2)}) collective-permute-start(bf16[2,128,256]{2,1,0:T(8,128)(2,1)S(1)} %get-tuple-element.77), channel_id=1, source_target_pairs={{0,4},{4,8},{8,12},{12,16},{16,20},{20,24},{24,28},{28,32},{32,36}... | collective-permute-start | bytes 393224 | tf_op jit(solution)/shard_map/ppermute | solution.py:25
  268.3 2.7 collective-permute-done.7
  274.2 2.5 fusion.21
  283.9 42.9 %all-reduce.9.cloned.1.call-done = (bf16[128,1024]{1,0:T(8,128)(2,1)}, bf16[512,1024]{1,0:T(8,128)(2,1)}) async-done(((bf16[128,1024]{1,0:T(8,128)(2,1)}, bf16[512,1024]{1,0:T(8,128)(2,1)}), (bf16[128,1024]{1,0:T(8,128)(2,1)}, bf16[512,1024]{1,0:T(8,128)(2,1)})) %all-reduce.9.cloned.1.call-update) | async-done | bytes 1310736 | tf_op jit(solution)/shard_map/psum | solution.py:328
  326.7 2.9 convert_element_type.278
  337.9 51.9 %shard_map.163 = f32[128,256]{1,0:T(8,128)S(1)} custom-call(bf16[2,4,8,128,256]{4,3,2,1,0:T(8,128)(2,1)S(1)} %bitcast.259), custom_call_target="tpu_custom_call" | custom-call | tf_op jit(solution)/shard_map/pallas_call | solution.py:178
  (286 shorter events, 106.3 us)
Async XLA Ops:
  7.2 110.6 %copy-start = (bf16[1024,256]{1,0:T(8,128)(2,1)S(1)}, bf16[1024,256]{1,0:T(8,128)(2,1)}, u32[]{:S(2)}) copy-start(bf16[1024,256]{1,0:T(8,128)(2,1)} %param.25) | copy-start | bytes 1572868
  7.2 68.6 %all-reduce.5.cloned.1.call-start = ((), (), s32[]{:S(2)}) async-start(), calls=%async_computation | async-start | bytes 524288 | tf_op jit(solution)/shard_map/psum | solution.py:241
  12.5 9.5 %collective-permute-start.1 = (bf16[2,128,256]{2,1,0:T(8,128)(2,1)S(1)}, bf16[2,128,256]{2,1,0:T(8,128)(2,1)S(1)}, u32[]{:S(2)}, u32[]{:S(2)}) collective-permute-start(bf16[2,128,256]{2,1,0:T(8,128)(2,1)S(1)} %pad_maximum_fusion.12), channel_id=1, source_target_pairs={{4,0},{8,4},{12,8},{16,12},{20,16},{24,20},{28,24},{32,28},{36,32}... | collective-permute-start | bytes 393224 | tf_op jit(solution)/shard_map/ppermute | solution.py:26
  17.7 4.3 %collective-permute-start = (bf16[2,128,256]{2,1,0:T(8,128)(2,1)S(1)}, bf16[2,128,256]{2,1,0:T(8,128)(2,1)S(1)}, u32[]{:S(2)}, u32[]{:S(2)}) collective-permute-start(bf16[2,128,256]{2,1,0:T(8,128)(2,1)S(1)} %pad_maximum_fusion.12), channel_id=1, source_target_pairs={{0,4},{4,8},{8,12},{12,16},{16,20},{20,24},{24,28},{28,32},{32,36}... | collective-permute-start | bytes 393224 | tf_op jit(solution)/shard_map/ppermute | solution.py:25
  21.3 96.4 %copy-start.53 = (f32[512]{0:T(512)}, f32[512]{0:T(512)S(1)}, u32[]{:S(2)}) copy-start(f32[512]{0:T(512)S(1)} %broadcast_multiply_fusion.6) | copy-start | bytes 6148
  24.5 55.3 %copy-start.35 = (bf16[4,64,128]{2,1,0:T(8,128)(2,1)}, bf16[4,64,128]{2,1,0:T(8,128)(2,1)S(1)}, u32[]{:S(2)}) copy-start(bf16[4,64,128]{2,1,0:T(8,128)(2,1)S(1)} %convolution_convert_fusion.14) | copy-start | bytes 196612
  25.9 217.4 %all-reduce.7.cloned.1.call-start = ((), (), s32[]{:S(2)}) async-start(), calls=%async_computation.1 | async-start | bytes 524288 | tf_op jit(solution)/shard_map/psum | solution.py:290
  25.9 91.8 %copy-start.51 = (f32[512]{0:T(512)}, f32[512]{0:T(512)S(1)}, u32[]{:S(2)}) copy-start(f32[512]{0:T(512)S(1)} %add_rsqrt_fusion) | copy-start | bytes 6148
  79.8 8.4 %collective-permute-start.3 = (bf16[2,128,256]{2,1,0:T(8,128)(2,1)S(1)}, bf16[2,128,256]{2,1,0:T(8,128)(2,1)S(1)}, u32[]{:S(2)}, u32[]{:S(2)}) collective-permute-start(bf16[2,128,256]{2,1,0:T(8,128)(2,1)S(1)} %pad_maximum_fusion.13), channel_id=1, source_target_pairs={{4,0},{8,4},{12,8},{16,12},{20,16},{24,20},{28,24},{32,28},{36,32}... | collective-permute-start | bytes 393224 | tf_op jit(solution)/shard_map/ppermute | solution.py:26
  84.6 4.9 %collective-permute-start.2 = (bf16[2,128,256]{2,1,0:T(8,128)(2,1)S(1)}, bf16[2,128,256]{2,1,0:T(8,128)(2,1)S(1)}, u32[]{:S(2)}, u32[]{:S(2)}) collective-permute-start(bf16[2,128,256]{2,1,0:T(8,128)(2,1)S(1)} %pad_maximum_fusion.13), channel_id=1, source_target_pairs={{0,4},{4,8},{8,12},{12,16},{16,20},{20,24},{24,28},{28,32},{32,36}... | collective-permute-start | bytes 393224 | tf_op jit(solution)/shard_map/ppermute | solution.py:25
  91.5 25.3 %copy-start.5 = (bf16[512,256]{1,0:T(8,128)(2,1)}, bf16[512,256]{1,0:T(8,128)(2,1)S(1)}, u32[]{:S(2)}) copy-start(bf16[512,256]{1,0:T(8,128)(2,1)S(1)} %gather_fusion.3) | copy-start | bytes 786436
  170.6 19.4 %collective-permute-start.4 = (bf16[2,128,256]{2,1,0:T(8,128)(2,1)}, bf16[2,128,256]{2,1,0:T(8,128)(2,1)}, u32[]{:S(2)}, u32[]{:S(2)}) collective-permute-start(bf16[2,128,256]{2,1,0:T(8,128)(2,1)} %get-tuple-element.79), channel_id=1, source_target_pairs={{0,4},{4,8},{8,12},{12,16},{16,20},{20,24},{24,28},{28,32},{32,36}... | collective-permute-start | bytes 393224 | tf_op jit(solution)/shard_map/ppermute | solution.py:25
  174.9 15.0 %collective-permute-start.5 = (bf16[2,128,256]{2,1,0:T(8,128)(2,1)}, bf16[2,128,256]{2,1,0:T(8,128)(2,1)}, u32[]{:S(2)}, u32[]{:S(2)}) collective-permute-start(bf16[2,128,256]{2,1,0:T(8,128)(2,1)} %get-tuple-element.80), channel_id=1, source_target_pairs={{4,0},{8,4},{12,8},{16,12},{20,16},{24,20},{28,24},{32,28},{36,32}... | collective-permute-start | bytes 393224 | tf_op jit(solution)/shard_map/ppermute | solution.py:26
  193.6 49.7 %copy-start.57 = (f32[128]{0:T(128)S(1)}, f32[128]{0:T(128)}, u32[]{:S(2)}) copy-start(f32[128]{0:T(128)} %copy-done.56) | copy-start | bytes 1540
  193.6 49.7 %copy-start.62 = (f32[128]{0:T(128)S(1)}, f32[128]{0:T(128)}, u32[]{:S(2)}) copy-start(f32[128]{0:T(128)} %copy-done.61) | copy-start | bytes 1540
  193.6 133.1 %all-reduce.9.cloned.1.call-start = ((), (), s32[]{:S(2)}) async-start(), calls=%async_computation.2 | async-start | bytes 2621440 | tf_op jit(solution)/shard_map/psum | solution.py:328
  196.9 51.7 %copy-start.29 = (bf16[1,384,256]{1,2,0:T(8,128)(2,1)S(1)}, bf16[1,384,256]{1,2,0:T(8,128)(2,1)}, u32[]{:S(2)}) copy-start(bf16[1,384,256]{1,2,0:T(8,128)(2,1)} %copy-done.28) | copy-start | bytes 589828
  196.9 51.7 %copy-start.34 = (bf16[128,256]{0,1:T(8,128)(2,1)S(1)}, bf16[128,256]{0,1:T(8,128)(2,1)}, u32[]{:S(2)}) copy-start(bf16[128,256]{0,1:T(8,128)(2,1)} %copy-done.33) | copy-start | bytes 196612
  257.7 13.3 %copy-start.4 = (f32[1,384,256]{2,1,0:T(8,128)S(1)}, f32[1,384,256]{2,1,0:T(8,128)}, u32[]{:S(2)}) copy-start(f32[1,384,256]{2,1,0:T(8,128)} %copy.108) | copy-start | bytes 1179652
  257.7 13.3 %copy-start.13 = (bf16[3,1024,256]{2,1,0:T(8,128)(2,1)S(1)}, bf16[3,1024,256]{2,1,0:T(8,128)(2,1)}, u32[]{:S(2)}) copy-start(bf16[3,1024,256]{2,1,0:T(8,128)(2,1)} %param.23) | copy-start | bytes 4718596
  259.0 9.4 %collective-permute-start.6 = (bf16[2,128,256]{2,1,0:T(8,128)(2,1)S(1)}, bf16[2,128,256]{2,1,0:T(8,128)(2,1)S(1)}, u32[]{:S(2)}, u32[]{:S(2)}) collective-permute-start(bf16[2,128,256]{2,1,0:T(8,128)(2,1)S(1)} %get-tuple-element.77), channel_id=1, source_target_pairs={{0,4},{4,8},{8,12},{12,16},{16,20},{20,24},{24,28},{28,32},{32,36}... | collective-permute-start | bytes 393224 | tf_op jit(solution)/shard_map/ppermute | solution.py:25
  264.8 6.3 %collective-permute-start.7 = (bf16[2,128,256]{2,1,0:T(8,128)(2,1)S(1)}, bf16[2,128,256]{2,1,0:T(8,128)(2,1)S(1)}, u32[]{:S(2)}, u32[]{:S(2)}) collective-permute-start(bf16[2,128,256]{2,1,0:T(8,128)(2,1)S(1)} %get-tuple-element.78), channel_id=1, source_target_pairs={{4,0},{8,4},{12,8},{16,12},{20,16},{24,20},{28,24},{32,28},{36,32}... | collective-permute-start | bytes 393224 | tf_op jit(solution)/shard_map/ppermute | solution.py:26
  280.9 48.7 %copy-start.52 = (f32[512]{0:T(512)S(1)}, f32[512]{0:T(512)}, u32[]{:S(2)}) copy-start(f32[512]{0:T(512)} %copy-done.51) | copy-start | bytes 6148
  280.9 48.7 %copy-start.54 = (f32[512]{0:T(512)S(1)}, f32[512]{0:T(512)}, u32[]{:S(2)}) copy-start(f32[512]{0:T(512)} %copy-done.53) | copy-start | bytes 6148
  (61 other events, 253.4 us)
Sparse Core Ops, SparseCore 0:
  26.0 49.7 all-reduce.4
  193.7 49.5 all-reduce.6
  272.9 53.7 all-reduce.8

commit v2 on v0

v2 whole, which is shorter than its diff:
```python
import jax
import jax.numpy as jnp
from jax import lax
from jax.experimental import pallas as pl
from jax.experimental.pallas import tpu as pltpu
from jax.sharding import PartitionSpec as P

NZ, NX, NC, NY = 8, 4, 2, 4
BANDS = NZ * NX * NC
D = 1024
ROWS = 128
POINTS = 512
COLS = 256
HEADS = 4
HEAD_DIM = 64
EDGES = 4
RIM = 16
WINDOW = 128
SHARE = ROWS // NY
PART = D // BANDS
EPS = 1e-05
NEG = -1e30
FACTOR = HEAD_DIM**-0.5
F32 = jnp.float32
BF16 = jnp.bfloat16
MESH = pl.DeviceIdType.MESH
GROUPS = (4, 2, 2)
REMOTE = 96


def dot_nn(a, b):
    return lax.dot_general(a, b, (((1,), (0,)), ((), ())), preferred_element_type=F32)


def dot_nt(a, b):
    return lax.dot_general(a, b, (((1,), (1,)), ((), ())), preferred_element_type=F32)


def dot_tn(a, b):
    return lax.dot_general(a, b, (((0,), (0,)), ((), ())), preferred_element_type=F32)


def normalise(values):
    values = values.astype(F32)
    centre = jnp.mean(values, axis=-1, keepdims=True)
    shifted = values - centre
    rstd = lax.rsqrt(jnp.mean(shifted * shifted, axis=-1, keepdims=True) + EPS)
    return shifted * rstd, rstd


def normalise_back(normed, rstd, upstream):
    first = jnp.mean(upstream, axis=-1, keepdims=True)
    second = jnp.mean(upstream * normed, axis=-1, keepdims=True)
    return rstd * (upstream - first - normed * second)


def head_masks(dtype):
    lane = lax.broadcasted_iota(jnp.int32, (1, COLS), 1)
    return [((lane >= h * HEAD_DIM) & (lane < (h + 1) * HEAD_DIM)).astype(F32).astype(dtype) for h in range(HEADS)]


def kernel(
    mesh_hbm, grid_hbm, dout_hbm, near_hbm, count_hbm, wqkv_hbm, wpo_hbm, wdq_hbm, wdkv_hbm, wdo_hbm,
    out_mesh, out_grid, out_qkv, out_po, out_dq, out_dkv, out_do,
    mesh_v, grid_v, dout_v, near_v, count_v, wqkv, wpo, wdq, wdkv, wdo,
    xhat, mn, mn_t, sn_t, sg_t, kv, qp, kbd, vbd, pt, dpt, attended,
    part1, part1_in, sn, gn, gn_t, dout_t, grstd, qd, ud,
    own_kv, rim_in, kbd_c, vbd_c, kbd_r, vbd_r, cc, cr, s_c, s_r, dw_c, dw_r, w_c, w_r, ds_c, ds_r,
    rim_out, rim_back, dkv_own, dec, dq, gb, gb_in, gstat, gstat_in,
    part2, part2_in, sgrad, sg, ring_out, ring_in, dqkv, part3, part3_in, back,
    g1, g2, g3, ra1, ra2, ra3, hb1, hb2, hb3, rb1, rb2, rb3, hc1, hc2, hc3, rc1, rc2, rc3,
    load_sem, send_sem, recv_sem,
):
    band = lax.axis_index("band")
    y = lax.axis_index("chan")
    core = lax.rem(band, NC)
    x = lax.rem(lax.div(band, NC), NX)
    z = lax.div(band, NC * NX)

    def at(zz, xx, c):
        return {"band": (zz * NX + xx) * NC + c}

    pair = at(z, x, 1 - core)
    x_peers = [at(z, lax.rem(x + d, NX), core) for d in range(1, NX)]
    z_peers = [at(lax.rem(z + d, NZ), x, core) for d in range(1, NZ)]
    y_peers = [{"chan": lax.rem(y + d, NY)} for d in range(1, NY)]
    above = {"band": lax.rem(band + 1, BANDS)}
    below = {"band": lax.rem(band + BANDS - 1, BANDS)}

    barrier = pltpu.get_barrier_semaphore()
    peers = [pair, above, below] + x_peers + y_peers + z_peers
    for peer in peers:
        pl.semaphore_signal(barrier, inc=1, device_id=peer, device_id_type=MESH)

    loads = []
    for i, (src, dst) in enumerate((
        (mesh_hbm, mesh_v), (wqkv_hbm, wqkv), (grid_hbm, grid_v), (wdq_hbm, wdq), (dout_hbm, dout_v), (wdo_hbm, wdo),
        (near_hbm, near_v), (count_hbm, count_v), (wpo_hbm, wpo), (wdkv_hbm, wdkv),
    )):
        load = pltpu.make_async_copy(src, dst, load_sem.at[i])
        load.start()
        loads.append(load)
    l_mesh, l_qkv, l_grid, l_dq, l_dout, l_do, l_near, l_count, l_po, l_dkv = loads

    used = []

    def push(src, dst, peer):
        slot = len(used)
        copy = pltpu.make_async_remote_copy(
            src_ref=src, dst_ref=dst, send_sem=send_sem.at[slot], recv_sem=recv_sem.at[slot],
            device_id=peer, device_id_type=MESH,
        )
        copy.start()
        used.append(copy)
        return copy

    def arrive(copies):
        for copy in copies:
            copy.wait_recv()

    masks = head_masks(BF16)
    masks_f = head_masks(F32)

    def scatter_share(partial, landing):
        return [push(partial.at[lax.rem(y + d, NY)], landing.at[d - 1], y_peers[d - 1]) for d in range(1, NY)]

    def gather_share(blocks):
        return [push(blocks.at[y], blocks.at[y], y_peers[d - 1]) for d in range(1, NY)]

    def share_sum(partial, landing):
        total = partial[y].astype(F32)
        for d in range(NY - 1):
            total = total + landing[d].astype(F32)
        return total

    def store_grad(group, first, left_t, right):
        width = right.shape[1] // COLS

        def rows(zz, carry):
            lhs = left_t[pl.ds(pl.multiple_of(zz * ROWS, ROWS), ROWS), :]
            value = dot_nn(lhs, right).astype(BF16)
            for xx in range(NX):
                for c in range(NC):
                    lo = (xx * NC + c) * PART
                    for m in range(width):
                        group[c, xx, zz, (first + m) * PART : (first + m + 1) * PART, :] = value[
                            lo : lo + PART, m * COLS : (m + 1) * COLS
                        ]
            return carry

        lax.fori_loop(0, NZ, rows, 0)

    def send_pair(group, landing):
        return [push(group.at[1 - core], landing, pair)]

    def add_pair(group, landing, half):
        def step(i, carry):
            xx, zz = lax.div(i, NZ), lax.rem(i, NZ)
            half[xx, zz] = (group[core, xx, zz].astype(F32) + landing[xx, zz].astype(F32)).astype(BF16)
            return carry

        lax.fori_loop(0, NX * NZ, step, 0)

    def send_x(half, landing):
        return [push(half.at[lax.rem(x + d, NX)], landing.at[d - 1], x_peers[d - 1]) for d in range(1, NX)]

    def add_x(half, landing, eighth):
        def step(zz, carry):
            total = half[x, zz].astype(F32)
            for d in range(NX - 1):
                total = total + landing[d, zz].astype(F32)
            eighth[zz] = total.astype(BF16)
            return carry

        lax.fori_loop(0, NZ, step, 0)

    def send_z(eighth, landing):
        return [push(eighth.at[lax.rem(z + d, NZ)], landing.at[d - 1], z_peers[d - 1]) for d in range(1, NZ)]

    def total_z(eighth, landing):
        total = eighth[z].astype(F32)
        for d in range(NZ - 1):
            total = total + landing[d].astype(F32)
        return total

    l_mesh.wait()
    xh, rstd_x = normalise(mesh_v[...])
    xhat[...] = xh
    mn[...] = xh.astype(BF16)
    l_qkv.wait()
    kv[1, 0] = dot_nn(mn[...], wqkv[1]).astype(BF16)
    kv[1, 1] = dot_nn(mn[...], wqkv[2]).astype(BF16)
    pl.semaphore_wait(barrier, len(peers))
    kv_copies = [push(kv.at[1], kv.at[0], above), push(kv.at[1], kv.at[2], below)]
    qp[...] = dot_nn(mn[...], wqkv[0]).astype(BF16)

    l_grid.wait()

    def grid_rows(i, carry):
        rows = pl.ds(pl.multiple_of(i * 64, 64), 64)
        gh, rstd = normalise(grid_v[rows, :])
        gn[rows, :] = gh.astype(BF16)
        grstd[rows, :] = jnp.broadcast_to(rstd, (64, 128))
        return carry

    lax.fori_loop(0, POINTS // 64, grid_rows, 0)
    mn_t[...] = mn[...].T

    arrive(kv_copies)

    def stack_heads(block, h):
        kbd[h, block * ROWS : (block + 1) * ROWS, :] = kv[block, 0] * masks[h]
        vbd[h, block * ROWS : (block + 1) * ROWS, :] = kv[block, 1] * masks[h]

    for h in range(HEADS):
        for block in range(3):
            stack_heads(block, h)
    span = 3 * ROWS
    pt[...] = dot_nt(kbd[...].reshape(HEADS * span, COLS), qp[...]).reshape(HEADS, span, ROWS)
    key_row = lax.broadcasted_iota(jnp.int32, (span, ROWS), 0)
    query_row = lax.broadcasted_iota(jnp.int32, (span, ROWS), 1)
    position = band * ROWS - ROWS + key_row
    valid = (
        (key_row >= query_row) & (key_row <= query_row + 2 * WINDOW)
        & (position >= 0) & (position < BANDS * ROWS)
    )

    def window_softmax(h, carry):
        score = jnp.where(valid, pt[h] * FACTOR, NEG)
        weight = jnp.exp(score - jnp.max(score, axis=0, keepdims=True))
        pt[h] = weight / jnp.sum(weight, axis=0, keepdims=True)
        return carry

    lax.fori_loop(0, HEADS, window_softmax, 0)
    probs_b = pt[...].astype(BF16).reshape(HEADS * span, ROWS)
    attended[...] = dot_tn(probs_b, vbd[...].reshape(HEADS * span, COLS)).astype(BF16)
    l_po.wait()
    part1[...] = dot_nn(attended[...], wpo[...]).astype(BF16).reshape(NY, SHARE, D)
    copies = scatter_share(part1, part1_in)

    l_dq.wait()
    qd[...] = dot_nn(gn[...], wdq[...]).astype(BF16)
    l_near.wait()
    l_count.wait()
    local = near_v[...] - band * ROWS
    count = count_v[...]

    def multiplicity(first, rows):
        mesh_row = lax.broadcasted_iota(jnp.int32, (rows, POINTS), 0) + first
        total = jnp.zeros((rows, POINTS), F32)
        for e in range(EDGES):
            hit = (local[e : e + 1] == mesh_row) & (count > e)
            total = total + jnp.where(hit, 1.0, 0.0)
        return total

    cc[...] = multiplicity(0, ROWS)
    cr[:RIM] = multiplicity(-RIM, RIM)
    cr[RIM:] = multiplicity(ROWS, RIM)

    arrive(copies)
    own_rows = pl.ds(pl.multiple_of(y * SHARE, SHARE), SHARE)
    state = (mesh_v[own_rows, :].astype(F32) + share_sum(part1, part1_in)).astype(BF16)
    yhat, rstd_y = normalise(state)
    sn[y] = yhat.astype(BF16)
    copies = gather_share(sn)

    l_dout.wait()
    l_do.wait()
    ud[...] = dot_nt(dout_v[...], wdo[...]).astype(BF16)
    l_dkv.wait()
    arrive(copies)

    state_normed = sn[...].reshape(ROWS, D)
    own_kv[0] = dot_nn(state_normed, wdkv[0]).astype(BF16)
    own_kv[1] = dot_nn(state_normed, wdkv[1]).astype(BF16)
    rim_copies = [
        push(own_kv.at[:, pl.ds(ROWS - RIM, RIM), :], rim_in.at[0], above),
        push(own_kv.at[:, pl.ds(0, RIM), :], rim_in.at[1], below),
    ]
    for h in range(HEADS):
        kbd_c[h] = own_kv[0] * masks[h]
        vbd_c[h] = own_kv[1] * masks[h]
    s_c[...] = dot_nt(kbd_c[...].reshape(HEADS * ROWS, COLS), qd[...]).reshape(HEADS, ROWS, POINTS)
    dw_c[...] = dot_nt(vbd_c[...].reshape(HEADS * ROWS, COLS), ud[...]).reshape(HEADS, ROWS, POINTS)
    arrive(rim_copies)
    for h in range(HEADS):
        for side in range(2):
            kbd_r[h, side * RIM : (side + 1) * RIM, :] = rim_in[side, 0] * masks[h]
            vbd_r[h, side * RIM : (side + 1) * RIM, :] = rim_in[side, 1] * masks[h]
    s_r[...] = dot_nt(kbd_r[...].reshape(HEADS * 2 * RIM, COLS), qd[...]).reshape(HEADS, 2 * RIM, POINTS)
    dw_r[...] = dot_nt(vbd_r[...].reshape(HEADS * 2 * RIM, COLS), ud[...]).reshape(HEADS, 2 * RIM, POINTS)

    def edge_softmax(h, carry):
        for lo in range(0, POINTS, 128):
            at_c, at_r = cc[:, lo : lo + 128], cr[:, lo : lo + 128]
            score_c = jnp.where(at_c > 0, s_c[h, :, lo : lo + 128] * FACTOR, NEG)
            score_r = jnp.where(at_r > 0, s_r[h, :, lo : lo + 128] * FACTOR, NEG)
            top = jnp.maximum(jnp.max(score_c, axis=0, keepdims=True), jnp.max(score_r, axis=0, keepdims=True))
            e_c = at_c * jnp.exp(score_c - top)
            e_r = at_r * jnp.exp(score_r - top)
            scale = 1.0 / (jnp.sum(e_c, axis=0, keepdims=True) + jnp.sum(e_r, axis=0, keepdims=True))
            e_c = e_c * scale
            e_r = e_r * scale
            d_c = dw_c[h, :, lo : lo + 128]
            d_r = dw_r[h, :, lo : lo + 128]
            centre = jnp.sum(e_c * d_c, axis=0, keepdims=True) + jnp.sum(e_r * d_r, axis=0, keepdims=True)
            w_c[h, :, lo : lo + 128] = e_c.astype(BF16)
            w_r[h, :, lo : lo + 128] = e_r.astype(BF16)
            ds_c[h, :, lo : lo + 128] = (e_c * (d_c - centre) * FACTOR).astype(BF16)
            ds_r[h, :, lo : lo + 128] = (e_r * (d_r - centre) * FACTOR).astype(BF16)
        return carry

    lax.fori_loop(0, HEADS, edge_softmax, 0)

    def own_head(product, rows):
        blocks = product.reshape(HEADS, rows, COLS)
        total = lax.index_in_dim(blocks, 0, 0, keepdims=False) * masks_f[0]
        for h in range(1, HEADS):
            total = total + lax.index_in_dim(blocks, h, 0, keepdims=False) * masks_f[h]
        return total

    def flat(ref):
        return ref[...].reshape(ref.shape[0] * ref.shape[1], ref.shape[2])

    dkr = own_head(dot_nn(flat(ds_r), qd[...]), 2 * RIM).astype(BF16)
    dvr = own_head(dot_nn(flat(w_r), ud[...]), 2 * RIM).astype(BF16)
    for side in range(2):
        rim_out[side, 0] = dkr[side * RIM : (side + 1) * RIM]
        rim_out[side, 1] = dvr[side * RIM : (side + 1) * RIM]
    rim_copies = [push(rim_out.at[0], rim_back.at[0], below), push(rim_out.at[1], rim_back.at[1], above)]
    dk = own_head(dot_nn(flat(ds_c), qd[...]), ROWS)
    dv = own_head(dot_nn(flat(w_c), ud[...]), ROWS)
    arrive(rim_copies)

    def fold(middle, which):
        low = middle[:RIM] + rim_back[1, which].astype(F32)
        high = middle[ROWS - RIM :] + rim_back[0, which].astype(F32)
        return jnp.concatenate([low, middle[RIM : ROWS - RIM], high], axis=0).astype(BF16)

    dkv_own[:, :COLS] = fold(dk, 0)
    dkv_own[:, COLS:] = fold(dv, 1)
    part2[...] = (
        (dot_nt(dkv_own[:, :COLS], wdkv[0]) + dot_nt(dkv_own[:, COLS:], wdkv[1])).astype(BF16).reshape(NY, SHARE, D)
    )
    copies = scatter_share(part2, part2_in)

    dec[...] = (dot_tn(flat(w_c), flat(vbd_c)) + dot_tn(flat(w_r), flat(vbd_r))).astype(BF16)
    dq[...] = (dot_tn(flat(ds_c), flat(kbd_c)) + dot_tn(flat(ds_r), flat(kbd_r))).astype(BF16)

    arrive(copies)
    sgrad[...] = normalise_back(yhat, rstd_y, share_sum(part2, part2_in))
    sg[y] = sgrad[...].astype(BF16)
    copies = gather_share(sg)

    dout_t[...] = dout_v[...].T
    gn_t[...] = gn[...].T
    store_grad(g1, 0, gn_t, dq[...])
    store_grad(g1, 1, dout_t, dec[...])
    sn_t[...] = state_normed.T
    store_grad(g1, 2, sn_t, dkv_own[...])
    pair1 = send_pair(g1, ra1)

    arrive(copies)
    state_grad_b = sg[...].reshape(ROWS, D)
    da = dot_nt(state_grad_b, wpo[...]).astype(BF16)
    dpt[...] = dot_nt(vbd[...].reshape(HEADS * span, COLS), da).reshape(HEADS, span, ROWS)

    def window_back(h, carry):
        prob = pt[h]
        dprob = dpt[h]
        centre = jnp.sum(prob * dprob, axis=0, keepdims=True)
        dpt[h] = prob * (dprob - centre)
        return carry

    lax.fori_loop(0, HEADS, window_back, 0)
    dscore = dpt[...].astype(BF16).reshape(HEADS * span, ROWS)
    dk_ext = own_head(dot_nn(dscore, qp[...]), span) * FACTOR
    dv_ext = own_head(dot_nn(pt[...].astype(BF16).reshape(HEADS * span, ROWS), da), span)
    ring_out[0, 0] = dk_ext[:ROWS].astype(BF16)
    ring_out[0, 1] = dv_ext[:ROWS].astype(BF16)
    ring_out[1, 0] = dk_ext[2 * ROWS :].astype(BF16)
    ring_out[1, 1] = dv_ext[2 * ROWS :].astype(BF16)
    ring_copies = [push(ring_out.at[0], ring_in.at[0], below), push(ring_out.at[1], ring_in.at[1], above)]
    dqkv[:, :COLS] = (
        dot_tn(dscore, kbd[...].reshape(HEADS * span, COLS)) * FACTOR
    ).astype(BF16)

    arrive(pair1)
    add_pair(g1, ra1, hb1)
    x1 = send_x(hb1, rb1)

    store_grad(g2, 0, mn_t, dqkv[:, :COLS])
    sg_t[...] = state_grad_b.T
    store_grad(g2, 1, sg_t, attended[...])
    pair2 = send_pair(g2, ra2)

    arrive(ring_copies)
    for which, ext in ((0, dk_ext), (1, dv_ext)):
        total = ext[ROWS : 2 * ROWS] + ring_in[0, which].astype(F32) + ring_in[1, which].astype(F32)
        dqkv[:, (which + 1) * COLS : (which + 2) * COLS] = total.astype(BF16)
    part3[...] = (
        (
            dot_nt(dqkv[:, :COLS], wqkv[0])
            + dot_nt(dqkv[:, COLS : 2 * COLS], wqkv[1])
            + dot_nt(dqkv[:, 2 * COLS :], wqkv[2])
        ).astype(BF16).reshape(NY, SHARE, D)
    )
    copies = scatter_share(part3, part3_in)
    store_grad(g3, 0, mn_t, dqkv[:, COLS:])
    pair3 = send_pair(g3, ra3)

    arrive(pair2)
    add_pair(g2, ra2, hb2)
    x2 = send_x(hb2, rb2)

    arrive(copies)
    own_x = xhat[own_rows, :]
    centred, rstd_own = normalise(mesh_v[own_rows, :])
    result = sgrad[...] + normalise_back(own_x, rstd_own, share_sum(part3, part3_in))
    back[y] = result.astype(BF16)
    back_copies = gather_share(back)

    arrive(pair3)
    add_pair(g3, ra3, hb3)
    x3 = send_x(hb3, rb3)

    def grid_part(i, carry):
        rows = pl.ds(pl.multiple_of(i * 128, 128), 128)
        value = dot_nt(dq[rows, :], wdq[...])
        first = jnp.mean(value, axis=-1, keepdims=True)
        second = jnp.mean(value * gn[rows, :].astype(F32), axis=-1, keepdims=True)
        lane = lax.broadcasted_iota(jnp.int32, (128, 128), 1)
        both = jnp.where(lane == 0, first, jnp.where(lane == 1, second, 0.0)).T
        gstat[i] = both[:8]
        for q in range(NY):
            gb[q, rows, :] = value[:, q * COLS : (q + 1) * COLS].astype(BF16)
        return carry

    lax.fori_loop(0, POINTS // 128, grid_part, 0)
    grid_copies = []
    for d in range(1, NY):
        grid_copies.append(push(gb.at[lax.rem(y + d, NY)], gb_in.at[d - 1], y_peers[d - 1]))
        grid_copies.append(push(gstat, gstat_in.at[d - 1], y_peers[d - 1]))

    arrive(x1)
    add_x(hb1, rb1, hc1)
    z1 = send_z(hc1, rc1)
    arrive(x2)
    add_x(hb2, rb2, hc2)
    z2 = send_z(hc2, rc2)
    arrive(x3)
    add_x(hb3, rb3, hc3)
    z3 = send_z(hc3, rc3)

    arrive(grid_copies)
    columns = pl.ds(pl.multiple_of(y * COLS, COLS), COLS)

    def grid_final(i, carry):
        rows = pl.ds(pl.multiple_of(i * 128, 128), 128)
        stat = gstat[i]
        value = gb[y, rows, :].astype(F32)
        for d in range(NY - 1):
            stat = stat + gstat_in[d, i]
            value = value + gb_in[d, rows, :].astype(F32)
        stat = jnp.concatenate([stat, jnp.zeros((120, 128), F32)], axis=0).T
        change = value - stat[:, 0:1] - gn[rows, columns].astype(F32) * stat[:, 1:2]
        out_grid[rows, :] = (dout_v[rows, columns].astype(F32) + grstd[rows, 0:1] * change).astype(BF16)
        return carry

    lax.fori_loop(0, POINTS // 128, grid_final, 0)
    arrive(back_copies)
    out_mesh[...] = back[...].reshape(ROWS, D)

    arrive(z1)
    total = total_z(hc1, rc1)
    out_dq[...] = total[:PART]
    out_do[...] = total[PART : 2 * PART]
    out_dkv[0] = total[2 * PART : 3 * PART]
    out_dkv[1] = total[3 * PART :]
    arrive(z2)
    total = total_z(hc2, rc2)
    out_qkv[0] = total[:PART]
    out_po[...] = total[PART:]
    arrive(z3)
    total = total_z(hc3, rc3)
    out_qkv[1] = total[:PART]
    out_qkv[2] = total[PART:]
    for copy in used:
        copy.wait_send()


def body(
    mesh_node_state, grid_state, d_out, neighbours, edge_count, w_proc_qkv, w_proc_out, w_dec_q, w_dec_kv, w_dec_out
):
    span = 3 * ROWS
    v = pltpu.VMEM

    def reduce_scratch(make):
        return [make(n * PART) for n in GROUPS]

    scratch = [
        v((ROWS, D), BF16), v((POINTS, D), BF16), v((POINTS, D), BF16), v((EDGES, POINTS), jnp.int32),
        v((1, POINTS), jnp.int32), v((3, D, COLS), BF16), v((COLS, D), BF16), v((D, COLS), BF16),
        v((2, D, COLS), BF16), v((COLS, D), BF16),
        v((ROWS, D), F32), v((ROWS, D), BF16), v((D, ROWS), BF16), v((D, ROWS), BF16), v((D, ROWS), BF16), v((3, 2, ROWS, COLS), BF16), v((ROWS, COLS), BF16),
        v((HEADS, span, COLS), BF16), v((HEADS, span, COLS), BF16), v((HEADS, span, ROWS), F32),
        v((HEADS, span, ROWS), F32), v((ROWS, COLS), BF16),
        v((NY, SHARE, D), BF16), v((NY - 1, SHARE, D), BF16), v((NY, SHARE, D), BF16), v((POINTS, D), BF16),
        v((D, POINTS), BF16), v((D, POINTS), BF16), v((POINTS, 128), F32), v((POINTS, COLS), BF16),
        v((POINTS, COLS), BF16),
        v((2, ROWS, COLS), BF16), v((2, 2, RIM, COLS), BF16),
        v((HEADS, ROWS, COLS), BF16), v((HEADS, ROWS, COLS), BF16),
        v((HEADS, 2 * RIM, COLS), BF16), v((HEADS, 2 * RIM, COLS), BF16),
        v((ROWS, POINTS), F32), v((2 * RIM, POINTS), F32),
        v((HEADS, ROWS, POINTS), F32), v((HEADS, 2 * RIM, POINTS), F32),
        v((HEADS, ROWS, POINTS), F32), v((HEADS, 2 * RIM, POINTS), F32),
        v((HEADS, ROWS, POINTS), BF16), v((HEADS, 2 * RIM, POINTS), BF16),
        v((HEADS, ROWS, POINTS), BF16), v((HEADS, 2 * RIM, POINTS), BF16),
        v((2, 2, RIM, COLS), BF16), v((2, 2, RIM, COLS), BF16), v((ROWS, 2 * COLS), BF16),
        v((POINTS, COLS), BF16), v((POINTS, COLS), BF16), v((NY, POINTS, COLS), BF16),
        v((NY - 1, POINTS, COLS), BF16), v((POINTS // 128, 8, 128), F32), v((NY - 1, POINTS // 128, 8, 128), F32),
        v((NY, SHARE, D), BF16), v((NY - 1, SHARE, D), BF16), v((SHARE, D), F32), v((NY, SHARE, D), BF16),
        v((2, 2, ROWS, COLS), BF16), v((2, 2, ROWS, COLS), BF16), v((ROWS, 3 * COLS), BF16),
        v((NY, SHARE, D), BF16), v((NY - 1, SHARE, D), BF16), v((NY, SHARE, D), BF16),
    ]
    scratch += reduce_scratch(lambda r: v((NC, NX, NZ, r, COLS), BF16))
    scratch += reduce_scratch(lambda r: v((NX, NZ, r, COLS), BF16))
    scratch += reduce_scratch(lambda r: v((NX, NZ, r, COLS), BF16))
    scratch += reduce_scratch(lambda r: v((NX - 1, NZ, r, COLS), BF16))
    scratch += reduce_scratch(lambda r: v((NZ, r, COLS), BF16))
    scratch += reduce_scratch(lambda r: v((NZ - 1, r, COLS), BF16))
    scratch += [
        pltpu.SemaphoreType.DMA((10,)), pltpu.SemaphoreType.DMA((REMOTE,)), pltpu.SemaphoreType.DMA((REMOTE,)),
    ]
    shapes = (
        ((ROWS, D), BF16), ((POINTS, COLS), BF16), ((3, PART, COLS), F32), ((PART, COLS), F32),
        ((PART, COLS), F32), ((2, PART, COLS), F32), ((PART, COLS), F32),
    )
    mesh_grad, grid_grad, g_qkv, g_po, g_dq, g_dkv, g_do = pl.pallas_call(
        kernel,
        out_shape=[jax.ShapeDtypeStruct(shape, kind) for shape, kind in shapes],
        in_specs=[pl.BlockSpec(memory_space=pl.ANY)] * 10,
        out_specs=[pl.BlockSpec(memory_space=pltpu.VMEM)] * 7,
        scratch_shapes=scratch,
        compiler_params=pltpu.CompilerParams(
            collective_id=0, has_side_effects=True, vmem_limit_bytes=56 * 2**20
        ),
    )(
        mesh_node_state, grid_state, d_out, neighbours.T, edge_count.reshape(1, POINTS),
        w_proc_qkv, w_proc_out, w_dec_q, w_dec_kv, w_dec_out,
    )
    return mesh_grad, grid_grad, g_qkv, g_po.T, g_dq, g_dkv, g_do.T


def solution(mesh):
    placed = (
        P("band", None), P("band", None), P("band", None), P("band", None), P("band"),
        P(None, None, "chan"), P("chan", None), P(None, "chan"), P(None, None, "chan"), P("chan", None),
    )
    return jax.shard_map(
        body,
        mesh=mesh,
        in_specs=placed,
        out_specs=(
            P("band", None), P("band", "chan"), P(None, "band", "chan"), P("chan", "band"),
            P("band", "chan"), P(None, "band", "chan"), P("chan", "band"),
        ),
        check_vma=False,
    )
```

time: 1040 us -> 95 us (0.09)
  the two profiles are of different devices: /device:TPU:1 before, /device:TPU:4 now
where the time goes in v2:
time: 95 us; the launch traced here: 94.6 us
  Pallas kernels  83.8 us (88%)
  local copies, waits for them, and re-layouts  10.1 us (11%)
    pallas_call x1, Pallas kernels, body(): pl.pallas_call(kernel, out_shape=[jax.ShapeDtypeStruct(shape, kind) for s...  83.8 us
    unnamed x7, local copies, waits for them, and re-layouts  10.1 us

profile of v2, /device:TPU:4, one launch (start us, length us, event | category | flops | bytes accessed | tf_op | source)
XLA Modules:
  0.0 94.6 jit_solution(8476567477864374455)
XLA Ops:
  0.6 83.8 %shard_map.153 = (bf16[128,1024]{1,0:T(8,128)(2,1)}, bf16[512,256]{1,0:T(8,128)(2,1)}, f32[3,16,256]{2,1,0:T(8,128)}, f32[16,256]{1,0:T(8,128)}, f32[16,256]{1,0...) custom-call(bf16[128,1024]{1,0:T(8,128)(2,1)} %mesh_hbm.1, bf16[512,1024]{1,0:T(8,128)(2,1)} %grid_hbm.1, ...), custom_call_target="tpu_custom_call" | custom-call | tf_op jit(solution)/shard_map/pallas_call | solution.py:539
  84.5 1.7 %copy.24 = bf16[128,1024]{1,0:T(8,128)(2,1)} copy(bf16[128,1024]{1,0:T(8,128)(2,1)} %get-tuple-element.28) | data formatting | bytes 524288
  86.1 1.7 %copy.25 = bf16[512,256]{1,0:T(8,128)(2,1)} copy(bf16[512,256]{1,0:T(8,128)(2,1)} %get-tuple-element.29) | data formatting | bytes 524288
  87.8 1.4 %copy.26 = f32[3,16,256]{2,1,0:T(8,128)} copy(f32[3,16,256]{2,1,0:T(8,128)} %get-tuple-element.30) | data formatting | bytes 98304
  89.2 1.3 %copy.27 = f32[256,16]{0,1:T(8,128)} copy(f32[256,16]{0,1:T(8,128)} %bitcast.5) | data formatting | bytes 32768
  90.5 1.3 %copy.28 = f32[16,256]{1,0:T(8,128)} copy(f32[16,256]{1,0:T(8,128)} %get-tuple-element.32) | data formatting | bytes 32768
  91.9 1.4 %copy.29 = f32[2,16,256]{2,1,0:T(8,128)} copy(f32[2,16,256]{2,1,0:T(8,128)} %get-tuple-element.33) | data formatting | bytes 65536
  93.2 1.3 %copy.30 = f32[256,16]{0,1:T(8,128)} copy(f32[256,16]{0,1:T(8,128)} %bitcast.4) | data formatting | bytes 32768

commit v3 on v2

--- a/solution.py
+++ b/solution.py
@@ -24,8 +24,9 @@
 F32 = jnp.float32
 BF16 = jnp.bfloat16
 MESH = pl.DeviceIdType.MESH
-GROUPS = (4, 2, 2)
-REMOTE = 96
+GROUPS = (2, 2, 2, 2)
+HALF = NZ // 2
+REMOTE = 112
 
 
 def dot_nn(a, b):
@@ -63,13 +64,14 @@
     mesh_hbm, grid_hbm, dout_hbm, near_hbm, count_hbm, wqkv_hbm, wpo_hbm, wdq_hbm, wdkv_hbm, wdo_hbm,
     out_mesh, out_grid, out_qkv, out_po, out_dq, out_dkv, out_do,
     mesh_v, grid_v, dout_v, near_v, count_v, wqkv, wpo, wdq, wdkv, wdo,
-    xhat, mn, mn_t, sn_t, sg_t, kv, qp, kbd, vbd, pt, dpt, attended,
+    xhat, mn, mn_t, mn_own_t, sn_t, sg_t, kv, qp, kbd, vbd, pt, dpt, attended,
     part1, part1_in, sn, gn, gn_t, dout_t, grstd, qd, ud,
-    own_kv, rim_in, kbd_c, vbd_c, kbd_r, vbd_r, cc, cr, s_c, s_r, dw_c, dw_r, w_c, w_r, ds_c, ds_r,
-    rim_out, rim_back, dkv_own, dec, dq, gb, gb_in, gstat, gstat_in,
-    part2, part2_in, sgrad, sg, ring_out, ring_in, dqkv, part3, part3_in, back,
-    g1, g2, g3, ra1, ra2, ra3, hb1, hb2, hb3, rb1, rb2, rb3, hc1, hc2, hc3, rc1, rc2, rc3,
-    load_sem, send_sem, recv_sem,
+    own_kv, kbd_c, vbd_c, kbd_r, vbd_r, cc, cr, s_c, s_r, dw_c, dw_r, w_c, w_r, ds_c, ds_r,
+    dkv_ext, dec, dq, gb, gb_in, gstat, gstat_in,
+    part2, part2_in, rim2_in, share, sgrad, sg, ring_out, ring_in, dkv3, dqkv, part3, part3_in, back,
+    g0, g1, g2, g3, ra0, ra1, ra2, ra3, hb0, hb1, hb2, hb3, ry0, ry1, ry2, ry3,
+    rb0, rb1, rb2, rb3, hc0, hc1, hc2, hc3, rc0, rc1, rc2, rc3,
+    load_sem, send_sem, recv_sem, rim_send, rim_recv, rim2_send, rim2_recv,
 ):
     band = lax.axis_index("band")
     y = lax.axis_index("chan")
@@ -81,16 +83,31 @@
         return {"band": (zz * NX + xx) * NC + c}
 
     pair = at(z, x, 1 - core)
-    x_peers = [at(z, lax.rem(x + d, NX), core) for d in range(1, NX)]
+    x_peers = [at(z, lax.rem(x + d, NX), core) for d in (1, NX - 1)]
     z_peers = [at(lax.rem(z + d, NZ), x, core) for d in range(1, NZ)]
     y_peers = [{"chan": lax.rem(y + d, NY)} for d in range(1, NY)]
     above = {"band": lax.rem(band + 1, BANDS)}
     below = {"band": lax.rem(band + BANDS - 1, BANDS)}
 
+    lower = [{"band": (band + BANDS - 1) % BANDS, "chan": c} for c in range(NY)]
+    upper = [{"band": (band + 1) % BANDS, "chan": c} for c in range(NY)]
+
     barrier = pltpu.get_barrier_semaphore()
-    peers = [pair, above, below] + x_peers + y_peers + z_peers
-    for peer in peers:
-        pl.semaphore_signal(barrier, inc=1, device_id=peer, device_id_type=MESH)
+
+    def greet(peers):
+        for peer in peers:
+            pl.semaphore_signal(barrier, inc=1, device_id=peer, device_id_type=MESH)
+
+    peers = [pair, above, below, lower[NY - 1], upper[0]] + x_peers + y_peers + z_peers
+    greet(peers)
+
+    @pl.when(y == 0)
+    def _():
+        greet(lower)
+
+    @pl.when(y == NY - 1)
+    def _():
+        greet(upper)
 
     loads = []
     for i, (src, dst) in enumerate((
@@ -161,14 +178,38 @@
 
         lax.fori_loop(0, NX * NZ, step, 0)
 
-    def send_x(half, landing):
-        return [push(half.at[lax.rem(x + d, NX)], landing.at[d - 1], x_peers[d - 1]) for d in range(1, NX)]
+    right_x, left_x = at(z, lax.rem(x + 1, NX), core), at(z, lax.rem(x + NX - 1, NX), core)
+    to_right, to_left, across = lax.rem(x + 1, NX), lax.rem(x + NX - 1, NX), lax.rem(x + 2, NX)
+    near, far = pl.ds(0, HALF), pl.ds(HALF, HALF)
+
+    def send_x(half, relay, landing):
+        first = [
+            push(half.at[across, near], relay.at[0], right_x),
+            push(half.at[across, far], relay.at[1], left_x),
+        ]
+        second = [
+            push(half.at[to_right, far], landing.at[0, far], right_x),
+            push(half.at[to_left, near], landing.at[1, near], left_x),
+        ]
+        return first, second
+
+    def relay_x(first, second, half, relay, landing):
+        arrive(first)
+
+        def step(i, carry):
+            half[to_right, i] = (half[to_right, i].astype(F32) + relay[0, i].astype(F32)).astype(BF16)
+            half[to_left, HALF + i] = (half[to_left, HALF + i].astype(F32) + relay[1, i].astype(F32)).astype(BF16)
+            return carry
+
+        lax.fori_loop(0, HALF, step, 0)
+        return second + [
+            push(half.at[to_right, near], landing.at[0, near], right_x),
+            push(half.at[to_left, far], landing.at[1, far], left_x),
+        ]
 
     def add_x(half, landing, eighth):
         def step(zz, carry):
-            total = half[x, zz].astype(F32)
-            for d in range(NX - 1):
-                total = total + landing[d, zz].astype(F32)
+            total = half[x, zz].astype(F32) + landing[0, zz].astype(F32) + landing[1, zz].astype(F32)
             eighth[zz] = total.astype(BF16)
             return carry
 
@@ -186,13 +227,15 @@
     l_mesh.wait()
     xh, rstd_x = normalise(mesh_v[...])
     xhat[...] = xh
-    mn[...] = xh.astype(BF16)
+    mn[1] = xh.astype(BF16)
     l_qkv.wait()
-    kv[1, 0] = dot_nn(mn[...], wqkv[1]).astype(BF16)
-    kv[1, 1] = dot_nn(mn[...], wqkv[2]).astype(BF16)
-    pl.semaphore_wait(barrier, len(peers))
+    kv[1, 0] = dot_nn(mn[1], wqkv[1]).astype(BF16)
+    kv[1, 1] = dot_nn(mn[1], wqkv[2]).astype(BF16)
+    outer = lax.div(y, NY - 1) + lax.div(NY - 1 - y, NY - 1)
+    pl.semaphore_wait(barrier, len(peers) + NY * outer)
     kv_copies = [push(kv.at[1], kv.at[0], above), push(kv.at[1], kv.at[2], below)]
-    qp[...] = dot_nn(mn[...], wqkv[0]).astype(BF16)
+    mn_copies = [push(mn.at[1], mn.at[0], above), push(mn.at[1], mn.at[2], below)]
+    qp[...] = dot_nn(mn[1], wqkv[0]).astype(BF16)
 
     l_grid.wait()
 
@@ -204,7 +247,9 @@
         return carry
 
     lax.fori_loop(0, POINTS // 64, grid_rows, 0)
-    mn_t[...] = mn[...].T
+    l_dq.wait()
+    qd[...] = dot_nn(gn[...], wdq[...]).astype(BF16)
+    gn_t[...] = gn[...].T
 
     arrive(kv_copies)
 
@@ -238,8 +283,10 @@
     part1[...] = dot_nn(attended[...], wpo[...]).astype(BF16).reshape(NY, SHARE, D)
     copies = scatter_share(part1, part1_in)
 
-    l_dq.wait()
-    qd[...] = dot_nn(gn[...], wdq[...]).astype(BF16)
+    l_dout.wait()
+    l_do.wait()
+    ud[...] = dot_nt(dout_v[...], wdo[...]).astype(BF16)
+    dout_t[...] = dout_v[...].T
     l_near.wait()
     l_count.wait()
     local = near_v[...] - band * ROWS
@@ -264,29 +311,42 @@
     sn[y] = yhat.astype(BF16)
     copies = gather_share(sn)
 
-    l_dout.wait()
-    l_do.wait()
-    ud[...] = dot_nt(dout_v[...], wdo[...]).astype(BF16)
+    def rim_copy(c, side):
+        row, dst = ((0, RIM), (SHARE - RIM, 0))[side]
+        return pltpu.make_async_remote_copy(
+            src_ref=sn.at[y, pl.ds(row, RIM), :], dst_ref=sn.at[NY, pl.ds(dst, RIM), :],
+            send_sem=rim_send.at[c], recv_sem=rim_recv.at[side],
+            device_id=(lower, upper)[side][c], device_id_type=MESH,
+        )
+
+    @pl.when(y == 0)
+    def _():
+        for c in range(NY):
+            rim_copy(c, 0).start()
+
+    @pl.when(y == NY - 1)
+    def _():
+        for c in range(NY):
+            rim_copy(c, 1).start()
+
+    arrive(mn_copies)
+    mn_t[...] = mn[...].reshape(3 * ROWS, D).T
     l_dkv.wait()
     arrive(copies)
-
-    state_normed = sn[...].reshape(ROWS, D)
+    rim_copy(0, 0).wait_recv()
+    rim_copy(0, 1).wait_recv()
+
+    state_normed = sn[...].reshape(ROWS + 2 * RIM, D)
+    sn_t[...] = state_normed.T
     own_kv[0] = dot_nn(state_normed, wdkv[0]).astype(BF16)
     own_kv[1] = dot_nn(state_normed, wdkv[1]).astype(BF16)
-    rim_copies = [
-        push(own_kv.at[:, pl.ds(ROWS - RIM, RIM), :], rim_in.at[0], above),
-        push(own_kv.at[:, pl.ds(0, RIM), :], rim_in.at[1], below),
-    ]
     for h in range(HEADS):
-        kbd_c[h] = own_kv[0] * masks[h]
-        vbd_c[h] = own_kv[1] * masks[h]
+        kbd_c[h] = own_kv[0, :ROWS, :] * masks[h]
+        vbd_c[h] = own_kv[1, :ROWS, :] * masks[h]
+        kbd_r[h] = own_kv[0, ROWS:, :] * masks[h]
+        vbd_r[h] = own_kv[1, ROWS:, :] * masks[h]
     s_c[...] = dot_nt(kbd_c[...].reshape(HEADS * ROWS, COLS), qd[...]).reshape(HEADS, ROWS, POINTS)
     dw_c[...] = dot_nt(vbd_c[...].reshape(HEADS * ROWS, COLS), ud[...]).reshape(HEADS, ROWS, POINTS)
-    arrive(rim_copies)
-    for h in range(HEADS):
-        for side in range(2):
-            kbd_r[h, side * RIM : (side + 1) * RIM, :] = rim_in[side, 0] * masks[h]
-            vbd_r[h, side * RIM : (side + 1) * RIM, :] = rim_in[side, 1] * masks[h]
     s_r[...] = dot_nt(kbd_r[...].reshape(HEADS * 2 * RIM, COLS), qd[...]).reshape(HEADS, 2 * RIM, POINTS)
     dw_r[...] = dot_nt(vbd_r[...].reshape(HEADS * 2 * RIM, COLS), ud[...]).reshape(HEADS, 2 * RIM, POINTS)
 
@@ -322,45 +382,90 @@
     def flat(ref):
         return ref[...].reshape(ref.shape[0] * ref.shape[1], ref.shape[2])
 
-    dkr = own_head(dot_nn(flat(ds_r), qd[...]), 2 * RIM).astype(BF16)
-    dvr = own_head(dot_nn(flat(w_r), ud[...]), 2 * RIM).astype(BF16)
-    for side in range(2):
-        rim_out[side, 0] = dkr[side * RIM : (side + 1) * RIM]
-        rim_out[side, 1] = dvr[side * RIM : (side + 1) * RIM]
-    rim_copies = [push(rim_out.at[0], rim_back.at[0], below), push(rim_out.at[1], rim_back.at[1], above)]
-    dk = own_head(dot_nn(flat(ds_c), qd[...]), ROWS)
-    dv = own_head(dot_nn(flat(w_c), ud[...]), ROWS)
-    arrive(rim_copies)
-
-    def fold(middle, which):
-        low = middle[:RIM] + rim_back[1, which].astype(F32)
-        high = middle[ROWS - RIM :] + rim_back[0, which].astype(F32)
-        return jnp.concatenate([low, middle[RIM : ROWS - RIM], high], axis=0).astype(BF16)
-
-    dkv_own[:, :COLS] = fold(dk, 0)
-    dkv_own[:, COLS:] = fold(dv, 1)
+    for which, (upstream_c, upstream_r, right) in enumerate(((ds_c, ds_r, qd), (w_c, w_r, ud))):
+        cols = slice(which * COLS, (which + 1) * COLS)
+        dkv_ext[:ROWS, cols] = own_head(dot_nn(flat(upstream_c), right[...]), ROWS).astype(BF16)
+        dkv_ext[ROWS:, cols] = own_head(dot_nn(flat(upstream_r), right[...]), 2 * RIM).astype(BF16)
     part2[...] = (
-        (dot_nt(dkv_own[:, :COLS], wdkv[0]) + dot_nt(dkv_own[:, COLS:], wdkv[1])).astype(BF16).reshape(NY, SHARE, D)
+        (dot_nt(dkv_ext[:, :COLS], wdkv[0]) + dot_nt(dkv_ext[:, COLS:], wdkv[1]))
+        .astype(BF16).reshape(NY + 1, SHARE, D)
     )
     copies = scatter_share(part2, part2_in)
 
+    def rim2_copy(side, slot):
+        return pltpu.make_async_remote_copy(
+            src_ref=part2.at[NY, pl.ds(side * RIM, RIM), :], dst_ref=rim2_in.at[slot],
+            send_sem=rim2_send.at[side], recv_sem=rim2_recv.at[slot],
+            device_id=(lower[NY - 1], upper[0])[side], device_id_type=MESH,
+        )
+
+    rim2_copy(0, y).start()
+    rim2_copy(1, y).start()
+
     dec[...] = (dot_tn(flat(w_c), flat(vbd_c)) + dot_tn(flat(w_r), flat(vbd_r))).astype(BF16)
     dq[...] = (dot_tn(flat(ds_c), flat(kbd_c)) + dot_tn(flat(ds_r), flat(kbd_r))).astype(BF16)
 
+    store_grad(g0, 0, gn_t, dq[...])
+    store_grad(g0, 1, dout_t, dec[...])
+    pair0 = send_pair(g0, ra0)
+    store_grad(g1, 0, sn_t, dkv_ext[...])
+    pair1 = send_pair(g1, ra1)
+    arrive(pair0)
+    add_pair(g0, ra0, hb0)
+    x0 = send_x(hb0, ry0, rb0)
+
     arrive(copies)
-    sgrad[...] = normalise_back(yhat, rstd_y, share_sum(part2, part2_in))
+    share[...] = share_sum(part2, part2_in)
+
+    def rim_sum():
+        for c in range(NY):
+            rim2_copy(0, c).wait_recv()
+        total = rim2_in[0].astype(F32)
+        for c in range(1, NY):
+            total = total + rim2_in[c].astype(F32)
+        return total
+
+    @pl.when(y == 0)
+    def _():
+        share[:RIM, :] = share[:RIM, :] + rim_sum()
+
+    @pl.when(y == NY - 1)
+    def _():
+        share[SHARE - RIM :, :] = share[SHARE - RIM :, :] + rim_sum()
+
+    sgrad[...] = normalise_back(yhat, rstd_y, share[...])
     sg[y] = sgrad[...].astype(BF16)
     copies = gather_share(sg)
 
-    dout_t[...] = dout_v[...].T
-    gn_t[...] = gn[...].T
-    store_grad(g1, 0, gn_t, dq[...])
-    store_grad(g1, 1, dout_t, dec[...])
-    sn_t[...] = state_normed.T
-    store_grad(g1, 2, sn_t, dkv_own[...])
-    pair1 = send_pair(g1, ra1)
+    def grid_part(i, carry):
+        rows = pl.ds(pl.multiple_of(i * 128, 128), 128)
+        half_rows = pl.ds(pl.multiple_of(lax.rem(i, 2) * 128, 128), 128)
+        half = lax.div(i, 2)
+        value = dot_nt(dq[rows, :], wdq[...])
+        first = jnp.mean(value, axis=-1, keepdims=True)
+        second = jnp.mean(value * gn[rows, :].astype(F32), axis=-1, keepdims=True)
+        lane = lax.broadcasted_iota(jnp.int32, (128, 128), 1)
+        both = jnp.where(lane == 0, first, jnp.where(lane == 1, second, 0.0)).T
+        gstat[i] = both[:8]
+        for q in range(NY):
+            gb[half, q, half_rows, :] = value[:, q * COLS : (q + 1) * COLS].astype(BF16)
+        return carry
+
+    lax.fori_loop(0, POINTS // 128, grid_part, 0)
+
+    def send_grid(half):
+        return [
+            push(gb.at[half, lax.rem(y + d, NY)], gb_in.at[half, d - 1], y_peers[d - 1]) for d in range(1, NY)
+        ]
+
+    arrive(pair1)
+    add_pair(g1, ra1, hb1)
+    x1 = send_x(hb1, ry1, rb1)
+    x0 = relay_x(*x0, hb0, ry0, rb0)
 
     arrive(copies)
+    grid_copies = send_grid(0)
+    x1 = relay_x(*x1, hb1, ry1, rb1)
     state_grad_b = sg[...].reshape(ROWS, D)
     da = dot_nt(state_grad_b, wpo[...]).astype(BF16)
     dpt[...] = dot_nt(vbd[...].reshape(HEADS * span, COLS), da).reshape(HEADS, span, ROWS)
@@ -376,23 +481,29 @@
     dscore = dpt[...].astype(BF16).reshape(HEADS * span, ROWS)
     dk_ext = own_head(dot_nn(dscore, qp[...]), span) * FACTOR
     dv_ext = own_head(dot_nn(pt[...].astype(BF16).reshape(HEADS * span, ROWS), da), span)
-    ring_out[0, 0] = dk_ext[:ROWS].astype(BF16)
-    ring_out[0, 1] = dv_ext[:ROWS].astype(BF16)
-    ring_out[1, 0] = dk_ext[2 * ROWS :].astype(BF16)
-    ring_out[1, 1] = dv_ext[2 * ROWS :].astype(BF16)
+    for which, ext in ((0, dk_ext), (1, dv_ext)):
+        rounded = ext.astype(BF16)
+        dkv3[:, which * COLS : (which + 1) * COLS] = rounded
+        ring_out[0, which] = rounded[:ROWS]
+        ring_out[1, which] = rounded[2 * ROWS :]
     ring_copies = [push(ring_out.at[0], ring_in.at[0], below), push(ring_out.at[1], ring_in.at[1], above)]
+    store_grad(g2, 0, mn_t, dkv3[...])
+    pair2 = send_pair(g2, ra2)
     dqkv[:, :COLS] = (
         dot_tn(dscore, kbd[...].reshape(HEADS * span, COLS)) * FACTOR
     ).astype(BF16)
-
-    arrive(pair1)
-    add_pair(g1, ra1, hb1)
-    x1 = send_x(hb1, rb1)
-
-    store_grad(g2, 0, mn_t, dqkv[:, :COLS])
+    mn_own_t[...] = mn_t[:, ROWS : 2 * ROWS]
+    store_grad(g3, 0, mn_own_t, dqkv[:, :COLS])
     sg_t[...] = state_grad_b.T
-    store_grad(g2, 1, sg_t, attended[...])
-    pair2 = send_pair(g2, ra2)
+    store_grad(g3, 1, sg_t, attended[...])
+    pair3 = send_pair(g3, ra3)
+
+    arrive(pair2)
+    add_pair(g2, ra2, hb2)
+    x2 = send_x(hb2, ry2, rb2)
+    arrive(x0)
+    add_x(hb0, rb0, hc0)
+    z0 = send_z(hc0, rc0)
 
     arrive(ring_copies)
     for which, ext in ((0, dk_ext), (1, dv_ext)):
@@ -406,12 +517,16 @@
         ).astype(BF16).reshape(NY, SHARE, D)
     )
     copies = scatter_share(part3, part3_in)
-    store_grad(g3, 0, mn_t, dqkv[:, COLS:])
-    pair3 = send_pair(g3, ra3)
-
-    arrive(pair2)
-    add_pair(g2, ra2, hb2)
-    x2 = send_x(hb2, rb2)
+
+    arrive(pair3)
+    add_pair(g3, ra3, hb3)
+    x3 = send_x(hb3, ry3, rb3)
+    x2 = relay_x(*x2, hb2, ry2, rb2)
+
+    arrive(x1)
+    add_x(hb1, rb1, hc1)
+    z1 = send_z(hc1, rc1)
+    x3 = relay_x(*x3, hb3, ry3, rb3)
 
     arrive(copies)
     own_x = xhat[own_rows, :]
@@ -419,32 +534,10 @@
     result = sgrad[...] + normalise_back(own_x, rstd_own, share_sum(part3, part3_in))
     back[y] = result.astype(BF16)
     back_copies = gather_share(back)
-
-    arrive(pair3)
-    add_pair(g3, ra3, hb3)
-    x3 = send_x(hb3, rb3)
-
-    def grid_part(i, carry):
-        rows = pl.ds(pl.multiple_of(i * 128, 128), 128)
-        value = dot_nt(dq[rows, :], wdq[...])
-        first = jnp.mean(value, axis=-1, keepdims=True)
-        second = jnp.mean(value * gn[rows, :].astype(F32), axis=-1, keepdims=True)
-        lane = lax.broadcasted_iota(jnp.int32, (128, 128), 1)
-        both = jnp.where(lane == 0, first, jnp.where(lane == 1, second, 0.0)).T
-        gstat[i] = both[:8]
-        for q in range(NY):
-            gb[q, rows, :] = value[:, q * COLS : (q + 1) * COLS].astype(BF16)
-        return carry
-
-    lax.fori_loop(0, POINTS // 128, grid_part, 0)
-    grid_copies = []
+    grid_copies += send_grid(1)
     for d in range(1, NY):
-        grid_copies.append(push(gb.at[lax.rem(y + d, NY)], gb_in.at[d - 1], y_peers[d - 1]))
         grid_copies.append(push(gstat, gstat_in.at[d - 1], y_peers[d - 1]))
 
-    arrive(x1)
-    add_x(hb1, rb1, hc1)
-    z1 = send_z(hc1, rc1)
     arrive(x2)
     add_x(hb2, rb2, hc2)
     z2 = send_z(hc2, rc2)
@@ -458,10 +551,12 @@
     def grid_final(i, carry):
         rows = pl.ds(pl.multiple_of(i * 128, 128), 128)
         stat = gstat[i]
-        value = gb[y, rows, :].astype(F32)
+        half_rows = pl.ds(pl.multiple_of(lax.rem(i, 2) * 128, 128), 128)
+        half = lax.div(i, 2)
+        value = gb[half, y, half_rows, :].astype(F32)
         for d in range(NY - 1):
             stat = stat + gstat_in[d, i]
-            value = value + gb_in[d, rows, :].astype(F32)
+            value = value + gb_in[half, d, half_rows, :].astype(F32)
         stat = jnp.concatenate([stat, jnp.zeros((120, 128), F32)], axis=0).T
         change = value - stat[:, 0:1] - gn[rows, columns].astype(F32) * stat[:, 1:2]
         out_grid[rows, :] = (dout_v[rows, columns].astype(F32) + grstd[rows, 0:1] * change).astype(BF16)
@@ -471,22 +566,38 @@
     arrive(back_copies)
     out_mesh[...] = back[...].reshape(ROWS, D)
 
+    arrive(z0)
+    total = total_z(hc0, rc0)
+    out_dq[...] = total[:PART]
+    out_do[...] = total[PART:]
     arrive(z1)
     total = total_z(hc1, rc1)
-    out_dq[...] = total[:PART]
-    out_do[...] = total[PART : 2 * PART]
-    out_dkv[0] = total[2 * PART : 3 * PART]
-    out_dkv[1] = total[3 * PART :]
+    out_dkv[0] = total[:PART]
+    out_dkv[1] = total[PART:]
     arrive(z2)
     total = total_z(hc2, rc2)
+    out_qkv[1] = total[:PART]
+    out_qkv[2] = total[PART:]
+    arrive(z3)
+    total = total_z(hc3, rc3)
     out_qkv[0] = total[:PART]
     out_po[...] = total[PART:]
-    arrive(z3)
-    total = total_z(hc3, rc3)
-    out_qkv[1] = total[:PART]
-    out_qkv[2] = total[PART:]
+    rim2_copy(0, 0).wait_send()
+    rim2_copy(1, 0).wait_send()
+
+    @pl.when((y == 0) | (y == NY - 1))
+    def _():
+        for c in range(NY):
+            rim_copy(c, 0).wait_send()
+
     for copy in used:
         copy.wait_send()
+
+
+def copy_out(*refs):
+    count = len(refs) // 2
+    for source, target in zip(refs[:count], refs[count:]):
+        target[...] = source[...]
 
 
 def body(
@@ -502,13 +613,13 @@
         v((ROWS, D), BF16), v((POINTS, D), BF16), v((POINTS, D), BF16), v((EDGES, POINTS), jnp.int32),
         v((1, POINTS), jnp.int32), v((3, D, COLS), BF16), v((COLS, D), BF16), v((D, COLS), BF16),
         v((2, D, COLS), BF16), v((COLS, D), BF16),
-        v((ROWS, D), F32), v((ROWS, D), BF16), v((D, ROWS), BF16), v((D, ROWS), BF16), v((D, ROWS), BF16), v((3, 2, ROWS, COLS), BF16), v((ROWS, COLS), BF16),
+        v((ROWS, D), F32), v((3, ROWS, D), BF16), v((D, span), BF16), v((D, ROWS), BF16), v((D, ROWS + 2 * RIM), BF16), v((D, ROWS), BF16), v((3, 2, ROWS, COLS), BF16), v((ROWS, COLS), BF16),
         v((HEADS, span, COLS), BF16), v((HEADS, span, COLS), BF16), v((HEADS, span, ROWS), F32),
         v((HEADS, span, ROWS), F32), v((ROWS, COLS), BF16),
-        v((NY, SHARE, D), BF16), v((NY - 1, SHARE, D), BF16), v((NY, SHARE, D), BF16), v((POINTS, D), BF16),
+        v((NY, SHARE, D), BF16), v((NY - 1, SHARE, D), BF16), v((NY + 1, SHARE, D), BF16), v((POINTS, D), BF16),
         v((D, POINTS), BF16), v((D, POINTS), BF16), v((POINTS, 128), F32), v((POINTS, COLS), BF16),
         v((POINTS, COLS), BF16),
-        v((2, ROWS, COLS), BF16), v((2, 2, RIM, COLS), BF16),
+        v((2, ROWS + 2 * RIM, COLS), BF16),
         v((HEADS, ROWS, COLS), BF16), v((HEADS, ROWS, COLS), BF16),
         v((HEADS, 2 * RIM, COLS), BF16), v((HEADS, 2 * RIM, COLS), BF16),
         v((ROWS, POINTS), F32), v((2 * RIM, POINTS), F32),
@@ -516,27 +627,32 @@
         v((HEADS, ROWS, POINTS), F32), v((HEADS, 2 * RIM, POINTS), F32),
         v((HEADS, ROWS, POINTS), BF16), v((HEADS, 2 * RIM, POINTS), BF16),
         v((HEADS, ROWS, POINTS), BF16), v((HEADS, 2 * RIM, POINTS), BF16),
-        v((2, 2, RIM, COLS), BF16), v((2, 2, RIM, COLS), BF16), v((ROWS, 2 * COLS), BF16),
-        v((POINTS, COLS), BF16), v((POINTS, COLS), BF16), v((NY, POINTS, COLS), BF16),
-        v((NY - 1, POINTS, COLS), BF16), v((POINTS // 128, 8, 128), F32), v((NY - 1, POINTS // 128, 8, 128), F32),
-        v((NY, SHARE, D), BF16), v((NY - 1, SHARE, D), BF16), v((SHARE, D), F32), v((NY, SHARE, D), BF16),
-        v((2, 2, ROWS, COLS), BF16), v((2, 2, ROWS, COLS), BF16), v((ROWS, 3 * COLS), BF16),
+        v((ROWS + 2 * RIM, 2 * COLS), BF16),
+        v((POINTS, COLS), BF16), v((POINTS, COLS), BF16), v((2, NY, POINTS // 2, COLS), BF16),
+        v((2, NY - 1, POINTS // 2, COLS), BF16), v((POINTS // 128, 8, 128), F32), v((NY - 1, POINTS // 128, 8, 128), F32),
+        v((NY + 1, SHARE, D), BF16), v((NY - 1, SHARE, D), BF16), v((NY, RIM, D), BF16), v((SHARE, D), F32),
+        v((SHARE, D), F32), v((NY, SHARE, D), BF16),
+        v((2, 2, ROWS, COLS), BF16), v((2, 2, ROWS, COLS), BF16),
+        v((span, 2 * COLS), BF16), v((ROWS, 3 * COLS), BF16),
         v((NY, SHARE, D), BF16), v((NY - 1, SHARE, D), BF16), v((NY, SHARE, D), BF16),
     ]
     scratch += reduce_scratch(lambda r: v((NC, NX, NZ, r, COLS), BF16))
     scratch += reduce_scratch(lambda r: v((NX, NZ, r, COLS), BF16))
     scratch += reduce_scratch(lambda r: v((NX, NZ, r, COLS), BF16))
-    scratch += reduce_scratch(lambda r: v((NX - 1, NZ, r, COLS), BF16))
+    scratch += reduce_scratch(lambda r: v((2, HALF, r, COLS), BF16))
+    scratch += reduce_scratch(lambda r: v((2, NZ, r, COLS), BF16))
     scratch += reduce_scratch(lambda r: v((NZ, r, COLS), BF16))
     scratch += reduce_scratch(lambda r: v((NZ - 1, r, COLS), BF16))
     scratch += [
         pltpu.SemaphoreType.DMA((10,)), pltpu.SemaphoreType.DMA((REMOTE,)), pltpu.SemaphoreType.DMA((REMOTE,)),
+        pltpu.SemaphoreType.DMA((NY,)), pltpu.SemaphoreType.DMA((2,)), pltpu.SemaphoreType.DMA((2,)),
+        pltpu.SemaphoreType.DMA((NY,)),
     ]
     shapes = (
         ((ROWS, D), BF16), ((POINTS, COLS), BF16), ((3, PART, COLS), F32), ((PART, COLS), F32),
         ((PART, COLS), F32), ((2, PART, COLS), F32), ((PART, COLS), F32),
     )
-    mesh_grad, grid_grad, g_qkv, g_po, g_dq, g_dkv, g_do = pl.pallas_call(
+    results = pl.pallas_call(
         kernel,
         out_shape=[jax.ShapeDtypeStruct(shape, kind) for shape, kind in shapes],
         in_specs=[pl.BlockSpec(memory_space=pl.ANY)] * 10,
@@ -549,6 +665,12 @@
         mesh_node_state, grid_state, d_out, neighbours.T, edge_count.reshape(1, POINTS),
         w_proc_qkv, w_proc_out, w_dec_q, w_dec_kv, w_dec_out,
     )
+    mesh_grad, grid_grad, g_qkv, g_po, g_dq, g_dkv, g_do = pl.pallas_call(
+        copy_out,
+        out_shape=[jax.ShapeDtypeStruct(shape, kind) for shape, kind in shapes],
+        in_specs=[pl.BlockSpec(memory_space=pltpu.VMEM)] * 7,
+        out_specs=[pl.BlockSpec(memory_space=pltpu.VMEM)] * 7,
+    )(*results)
     return mesh_grad, grid_grad, g_qkv, g_po.T, g_dq, g_dkv, g_do.T
 
 

time: 95 us -> 74.3 us (0.78)
  the two profiles are of different devices: /device:TPU:4 before, /device:TPU:1 now
where the time goes in v3:
time: 74.3 us; the launch traced here: 74.2 us
  Pallas kernels  73.6 us (99%)
    pallas_call x1, Pallas kernels, body(): pl.pallas_call(kernel, out_shape=[jax.ShapeDtypeStruct(shape, kind) for s...  71.7 us
    pallas_call x1, Pallas kernels, body(): pl.pallas_call(copy_out, out_shape=[jax.ShapeDtypeStruct(shape, kind) for...  1.91 us

profile of v3, /device:TPU:1, one launch (start us, length us, event | category | flops | bytes accessed | tf_op | source)
XLA Modules:
  0.0 74.2 jit_solution(17105383865874991171)
XLA Ops:
  0.6 71.7 %shard_map.153 = (bf16[128,1024]{1,0:T(8,128)(2,1)}, bf16[512,256]{1,0:T(8,128)(2,1)}, f32[3,16,256]{2,1,0:T(8,128)}, f32[16,256]{1,0:T(8,128)}, f32[16,256]{1,0...) custom-call(bf16[128,1024]{1,0:T(8,128)(2,1)} %mesh_hbm.1, bf16[512,1024]{1,0:T(8,128)(2,1)} %grid_hbm.1, ...), custom_call_target="tpu_custom_call" | custom-call | tf_op jit(solution)/shard_map/pallas_call | solution.py:655
  72.3 1.9 %shard_map.154 = (bf16[128,1024]{1,0:T(8,128)(2,1)}, bf16[512,256]{1,0:T(8,128)(2,1)}, f32[3,16,256]{2,1,0:T(8,128)}, f32[16,256]{1,0:T(8,128)}, f32[16,256]{1,0...) custom-call(bf16[128,1024]{1,0:T(8,128)(2,1)} %get-tuple-element.21.refs_0_, ...), custom_call_target="tpu_custom_call" | custom-call | tf_op jit(solution)/shard_map/pallas_call | solution.py:668

commit v4 on v3

--- a/solution.py
+++ b/solution.py
@@ -24,9 +24,9 @@
 F32 = jnp.float32
 BF16 = jnp.bfloat16
 MESH = pl.DeviceIdType.MESH
-GROUPS = (2, 2, 2, 2)
+GROUPS = (1, 2, 2, 1)
 HALF = NZ // 2
-REMOTE = 112
+REMOTE = 128
 
 
 def dot_nn(a, b):
@@ -71,6 +71,7 @@
     part2, part2_in, rim2_in, share, sgrad, sg, ring_out, ring_in, dkv3, dqkv, part3, part3_in, back,
     g0, g1, g2, g3, ra0, ra1, ra2, ra3, hb0, hb1, hb2, hb3, ry0, ry1, ry2, ry3,
     rb0, rb1, rb2, rb3, hc0, hc1, hc2, hc3, rc0, rc1, rc2, rc3,
+    ga, gq, raa, raq, hba, hbq, rza, rzq, hca, hcq, rxa, rxq,
     load_sem, send_sem, recv_sem, rim_send, rim_recv, rim2_send, rim2_recv,
 ):
     band = lax.axis_index("band")
@@ -83,7 +84,8 @@
         return {"band": (zz * NX + xx) * NC + c}
 
     pair = at(z, x, 1 - core)
-    x_peers = [at(z, lax.rem(x + d, NX), core) for d in (1, NX - 1)]
+    x_peers = [at(z, lax.rem(x + d, NX), core) for d in range(1, NX)]
+    across_x = x_peers[1]
     z_peers = [at(lax.rem(z + d, NZ), x, core) for d in range(1, NZ)]
     y_peers = [{"chan": lax.rem(y + d, NY)} for d in range(1, NY)]
     above = {"band": lax.rem(band + 1, BANDS)}
@@ -171,12 +173,36 @@
         return [push(group.at[1 - core], landing, pair)]
 
     def add_pair(group, landing, half):
-        def step(i, carry):
-            xx, zz = lax.div(i, NZ), lax.rem(i, NZ)
-            half[xx, zz] = (group[core, xx, zz].astype(F32) + landing[xx, zz].astype(F32)).astype(BF16)
+        def step(xx, carry):
+            for zz in range(NZ):
+                half[xx, zz] = group[core, xx, zz] + landing[xx, zz]
             return carry
 
-        lax.fori_loop(0, NX * NZ, step, 0)
+        lax.fori_loop(0, NX, step, 0)
+
+    def add_pair_z(group, landing, half):
+        def step(xx, carry):
+            for zz in range(NZ):
+                half[zz, xx] = group[core, xx, zz] + landing[xx, zz]
+            return carry
+
+        lax.fori_loop(0, NX, step, 0)
+
+    def add_z(half, landing, eighth):
+        for xx in range(NX):
+            total = half[z, xx].astype(F32)
+            for d in range(NZ - 1):
+                total = total + landing[d, xx].astype(F32)
+            eighth[xx] = total.astype(BF16)
+
+    def send_x_last(eighth, landing):
+        return [push(eighth.at[lax.rem(x + d, NX)], landing.at[d - 1], x_peers[d - 1]) for d in range(1, NX)]
+
+    def total_x(eighth, landing):
+        total = eighth[x].astype(F32)
+        for d in range(NX - 1):
+            total = total + landing[d].astype(F32)
+        return total
 
     right_x, left_x = at(z, lax.rem(x + 1, NX), core), at(z, lax.rem(x + NX - 1, NX), core)
     to_right, to_left, across = lax.rem(x + 1, NX), lax.rem(x + NX - 1, NX), lax.rem(x + 2, NX)
@@ -197,8 +223,8 @@
         arrive(first)
 
         def step(i, carry):
-            half[to_right, i] = (half[to_right, i].astype(F32) + relay[0, i].astype(F32)).astype(BF16)
-            half[to_left, HALF + i] = (half[to_left, HALF + i].astype(F32) + relay[1, i].astype(F32)).astype(BF16)
+            half[to_right, i] = half[to_right, i] + relay[0, i]
+            half[to_left, HALF + i] = half[to_left, HALF + i] + relay[1, i]
             return carry
 
         lax.fori_loop(0, HALF, step, 0)
@@ -206,6 +232,22 @@
             push(half.at[to_right, near], landing.at[0, near], right_x),
             push(half.at[to_left, far], landing.at[1, far], left_x),
         ]
+
+    def send_x_direct(half, relay, landing):
+        return [
+            push(half.at[to_right], landing.at[0], right_x),
+            push(half.at[to_left], landing.at[1], left_x),
+            push(half.at[across], relay, across_x),
+        ]
+
+    def add_x_direct(half, relay, landing, eighth):
+        def step(zz, carry):
+            total = half[x, zz].astype(F32) + landing[0, zz].astype(F32)
+            total = total + landing[1, zz].astype(F32) + relay[zz].astype(F32)
+            eighth[zz] = total.astype(BF16)
+            return carry
+
+        lax.fori_loop(0, NZ, step, 0)
 
     def add_x(half, landing, eighth):
         def step(zz, carry):
@@ -234,7 +276,6 @@
     outer = lax.div(y, NY - 1) + lax.div(NY - 1 - y, NY - 1)
     pl.semaphore_wait(barrier, len(peers) + NY * outer)
     kv_copies = [push(kv.at[1], kv.at[0], above), push(kv.at[1], kv.at[2], below)]
-    mn_copies = [push(mn.at[1], mn.at[0], above), push(mn.at[1], mn.at[2], below)]
     qp[...] = dot_nn(mn[1], wqkv[0]).astype(BF16)
 
     l_grid.wait()
@@ -252,6 +293,7 @@
     gn_t[...] = gn[...].T
 
     arrive(kv_copies)
+    mn_copies = [push(mn.at[1], mn.at[0], above), push(mn.at[1], mn.at[2], below)]
 
     def stack_heads(block, h):
         kbd[h, block * ROWS : (block + 1) * ROWS, :] = kv[block, 0] * masks[h]
@@ -405,14 +447,12 @@
     dec[...] = (dot_tn(flat(w_c), flat(vbd_c)) + dot_tn(flat(w_r), flat(vbd_r))).astype(BF16)
     dq[...] = (dot_tn(flat(ds_c), flat(kbd_c)) + dot_tn(flat(ds_r), flat(kbd_r))).astype(BF16)
 
-    store_grad(g0, 0, gn_t, dq[...])
-    store_grad(g0, 1, dout_t, dec[...])
+    store_grad(ga, 0, gn_t, dq[...])
+    paira = send_pair(ga, raa)
+    store_grad(g0, 0, dout_t, dec[...])
     pair0 = send_pair(g0, ra0)
     store_grad(g1, 0, sn_t, dkv_ext[...])
     pair1 = send_pair(g1, ra1)
-    arrive(pair0)
-    add_pair(g0, ra0, hb0)
-    x0 = send_x(hb0, ry0, rb0)
 
     arrive(copies)
     share[...] = share_sum(part2, part2_in)
@@ -436,6 +476,12 @@
     sgrad[...] = normalise_back(yhat, rstd_y, share[...])
     sg[y] = sgrad[...].astype(BF16)
     copies = gather_share(sg)
+    arrive(paira)
+    add_pair_z(ga, raa, hba)
+    za = send_z(hba, rza)
+    arrive(pair0)
+    add_pair(g0, ra0, hb0)
+    x0 = send_x(hb0, ry0, rb0)
 
     def grid_part(i, carry):
         rows = pl.ds(pl.multiple_of(i * 128, 128), 128)
@@ -487,23 +533,18 @@
         ring_out[0, which] = rounded[:ROWS]
         ring_out[1, which] = rounded[2 * ROWS :]
     ring_copies = [push(ring_out.at[0], ring_in.at[0], below), push(ring_out.at[1], ring_in.at[1], above)]
+    settled = len(used)
     store_grad(g2, 0, mn_t, dkv3[...])
     pair2 = send_pair(g2, ra2)
     dqkv[:, :COLS] = (
         dot_tn(dscore, kbd[...].reshape(HEADS * span, COLS)) * FACTOR
     ).astype(BF16)
     mn_own_t[...] = mn_t[:, ROWS : 2 * ROWS]
-    store_grad(g3, 0, mn_own_t, dqkv[:, :COLS])
+    store_grad(gq, 0, mn_own_t, dqkv[:, :COLS])
+    pairq = send_pair(gq, raq)
     sg_t[...] = state_grad_b.T
-    store_grad(g3, 1, sg_t, attended[...])
+    store_grad(g3, 0, sg_t, attended[...])
     pair3 = send_pair(g3, ra3)
-
-    arrive(pair2)
-    add_pair(g2, ra2, hb2)
-    x2 = send_x(hb2, ry2, rb2)
-    arrive(x0)
-    add_x(hb0, rb0, hc0)
-    z0 = send_z(hc0, rc0)
 
     arrive(ring_copies)
     for which, ext in ((0, dk_ext), (1, dv_ext)):
@@ -518,15 +559,15 @@
     )
     copies = scatter_share(part3, part3_in)
 
+    arrive(pair2)
+    add_pair(g2, ra2, hb2)
+    x2 = send_x_direct(hb2, ry2, rb2)
+    arrive(pairq)
+    add_pair_z(gq, raq, hbq)
+    zq = send_z(hbq, rzq)
     arrive(pair3)
     add_pair(g3, ra3, hb3)
-    x3 = send_x(hb3, ry3, rb3)
-    x2 = relay_x(*x2, hb2, ry2, rb2)
-
-    arrive(x1)
-    add_x(hb1, rb1, hc1)
-    z1 = send_z(hc1, rc1)
-    x3 = relay_x(*x3, hb3, ry3, rb3)
+    x3 = send_x_direct(hb3, ry3, rb3)
 
     arrive(copies)
     own_x = xhat[own_rows, :]
@@ -538,11 +579,26 @@
     for d in range(1, NY):
         grid_copies.append(push(gstat, gstat_in.at[d - 1], y_peers[d - 1]))
 
+    arrive(za)
+    add_z(hba, rza, hca)
+    xa = send_x_last(hca, rxa)
+    arrive(x0)
+    add_x(hb0, rb0, hc0)
+    z0 = send_z(hc0, rc0)
+    arrive(x1)
+    add_x(hb1, rb1, hc1)
+    z1 = send_z(hc1, rc1)
+
+    for copy in used[:settled]:
+        copy.wait_send()
     arrive(x2)
-    add_x(hb2, rb2, hc2)
+    add_x_direct(hb2, ry2, rb2, hc2)
     z2 = send_z(hc2, rc2)
+    arrive(zq)
+    add_z(hbq, rzq, hcq)
+    xq = send_x_last(hcq, rxq)
     arrive(x3)
-    add_x(hb3, rb3, hc3)
+    add_x_direct(hb3, ry3, rb3, hc3)
     z3 = send_z(hc3, rc3)
 
     arrive(grid_copies)
@@ -567,9 +623,9 @@
     out_mesh[...] = back[...].reshape(ROWS, D)
 
     arrive(z0)
-    total = total_z(hc0, rc0)
-    out_dq[...] = total[:PART]
-    out_do[...] = total[PART:]
+    out_do[...] = total_z(hc0, rc0)
+    arrive(xa)
+    out_dq[...] = total_x(hca, rxa)
     arrive(z1)
     total = total_z(hc1, rc1)
     out_dkv[0] = total[:PART]
@@ -578,10 +634,10 @@
     total = total_z(hc2, rc2)
     out_qkv[1] = total[:PART]
     out_qkv[2] = total[PART:]
+    arrive(xq)
+    out_qkv[0] = total_x(hcq, rxq)
     arrive(z3)
-    total = total_z(hc3, rc3)
-    out_qkv[0] = total[:PART]
-    out_po[...] = total[PART:]
+    out_po[...] = total_z(hc3, rc3)
     rim2_copy(0, 0).wait_send()
     rim2_copy(1, 0).wait_send()
 
@@ -590,7 +646,7 @@
         for c in range(NY):
             rim_copy(c, 0).wait_send()
 
-    for copy in used:
+    for copy in used[settled:]:
         copy.wait_send()
 
 
@@ -639,10 +695,14 @@
     scratch += reduce_scratch(lambda r: v((NC, NX, NZ, r, COLS), BF16))
     scratch += reduce_scratch(lambda r: v((NX, NZ, r, COLS), BF16))
     scratch += reduce_scratch(lambda r: v((NX, NZ, r, COLS), BF16))
-    scratch += reduce_scratch(lambda r: v((2, HALF, r, COLS), BF16))
+    scratch += reduce_scratch(lambda r: v((2, HALF, r, COLS), BF16))[:2]
+    scratch += reduce_scratch(lambda r: v((NZ, r, COLS), BF16))[2:]
     scratch += reduce_scratch(lambda r: v((2, NZ, r, COLS), BF16))
     scratch += reduce_scratch(lambda r: v((NZ, r, COLS), BF16))
     scratch += reduce_scratch(lambda r: v((NZ - 1, r, COLS), BF16))
+    chunk = (PART, COLS)
+    for lead in ((NC, NX, NZ), (NX, NZ), (NZ, NX), (NZ - 1, NX), (NX,), (NX - 1,)):
+        scratch += [v(lead + chunk, BF16), v(lead + chunk, BF16)]
     scratch += [
         pltpu.SemaphoreType.DMA((10,)), pltpu.SemaphoreType.DMA((REMOTE,)), pltpu.SemaphoreType.DMA((REMOTE,)),
         pltpu.SemaphoreType.DMA((NY,)), pltpu.SemaphoreType.DMA((2,)), pltpu.SemaphoreType.DMA((2,)),

time: 74.3 us -> 73.9 us (level)
  Pallas kernels: 73.6 us -> 72.7 us
    pallas_call x1, Pallas kernels: 71.7 us -> 70.8 us  [body(): pl.pallas_call(kernel, out_shape=[jax.ShapeDtypeStruct(shape, kind) for s...]
where the time goes in v4:
time: 73.9 us; the launch traced here: 73.4 us
  Pallas kernels  72.7 us (98%)
    pallas_call x1, Pallas kernels, body(): pl.pallas_call(kernel, out_shape=[jax.ShapeDtypeStruct(shape, kind) for s...  70.8 us
    pallas_call x1, Pallas kernels, body(): pl.pallas_call(copy_out, out_shape=[jax.ShapeDtypeStruct(shape, kind) for...  1.91 us

profile of v4, /device:TPU:1, one launch (start us, length us, event | category | flops | bytes accessed | tf_op | source)
XLA Modules:
  0.0 73.4 jit_solution(5983765685836320976)
XLA Ops:
  0.6 70.8 %shard_map.153 = (bf16[128,1024]{1,0:T(8,128)(2,1)}, bf16[512,256]{1,0:T(8,128)(2,1)}, f32[3,16,256]{2,1,0:T(8,128)}, f32[16,256]{1,0:T(8,128)}, f32[16,256]{1,0...) custom-call(bf16[128,1024]{1,0:T(8,128)(2,1)} %mesh_hbm.1, bf16[512,1024]{1,0:T(8,128)(2,1)} %grid_hbm.1, ...), custom_call_target="tpu_custom_call" | custom-call | tf_op jit(solution)/shard_map/pallas_call | solution.py:715
  71.5 1.9 %shard_map.154 = (bf16[128,1024]{1,0:T(8,128)(2,1)}, bf16[512,256]{1,0:T(8,128)(2,1)}, f32[3,16,256]{2,1,0:T(8,128)}, f32[16,256]{1,0:T(8,128)}, f32[16,256]{1,0...) custom-call(bf16[128,1024]{1,0:T(8,128)(2,1)} %get-tuple-element.21.refs_0_, ...), custom_call_target="tpu_custom_call" | custom-call | tf_op jit(solution)/shard_map/pallas_call | solution.py:728

commit v5 on v4

--- a/solution.py
+++ b/solution.py
@@ -546,6 +546,16 @@
     store_grad(g3, 0, sg_t, attended[...])
     pair3 = send_pair(g3, ra3)
 
+    arrive(pair2)
+    add_pair(g2, ra2, hb2)
+    x2 = send_x_direct(hb2, ry2, rb2)
+    arrive(pairq)
+    add_pair_z(gq, raq, hbq)
+    zq = send_z(hbq, rzq)
+    arrive(pair3)
+    add_pair(g3, ra3, hb3)
+    x3 = send_x_direct(hb3, ry3, rb3)
+
     arrive(ring_copies)
     for which, ext in ((0, dk_ext), (1, dv_ext)):
         total = ext[ROWS : 2 * ROWS] + ring_in[0, which].astype(F32) + ring_in[1, which].astype(F32)
@@ -558,16 +568,6 @@
         ).astype(BF16).reshape(NY, SHARE, D)
     )
     copies = scatter_share(part3, part3_in)
-
-    arrive(pair2)
-    add_pair(g2, ra2, hb2)
-    x2 = send_x_direct(hb2, ry2, rb2)
-    arrive(pairq)
-    add_pair_z(gq, raq, hbq)
-    zq = send_z(hbq, rzq)
-    arrive(pair3)
-    add_pair(g3, ra3, hb3)
-    x3 = send_x_direct(hb3, ry3, rb3)
 
     arrive(copies)
     own_x = xhat[own_rows, :]

time: 73.9 us -> 76.7 us (1.038)
  Pallas kernels: 72.7 us -> 76 us
    pallas_call x1, Pallas kernels: 70.8 us -> 74.1 us  [body(): pl.pallas_call(kernel, out_shape=[jax.ShapeDtypeStruct(shape, kind) for s...]
where the time goes in v5:
time: 76.7 us; the launch traced here: 76.6 us
  Pallas kernels  76 us (99%)
    pallas_call x1, Pallas kernels, body(): pl.pallas_call(kernel, out_shape=[jax.ShapeDtypeStruct(shape, kind) for s...  74.1 us
    pallas_call x1, Pallas kernels, body(): pl.pallas_call(copy_out, out_shape=[jax.ShapeDtypeStruct(shape, kind) for...  1.91 us

profile of v5, /device:TPU:1, one launch (start us, length us, event | category | flops | bytes accessed | tf_op | source)
XLA Modules:
  0.0 76.6 jit_solution(11698306197534440488)
XLA Ops:
  0.6 74.1 %shard_map.153 = (bf16[128,1024]{1,0:T(8,128)(2,1)}, bf16[512,256]{1,0:T(8,128)(2,1)}, f32[3,16,256]{2,1,0:T(8,128)}, f32[16,256]{1,0:T(8,128)}, f32[16,256]{1,0...) custom-call(bf16[128,1024]{1,0:T(8,128)(2,1)} %mesh_hbm.1, bf16[512,1024]{1,0:T(8,128)(2,1)} %grid_hbm.1, ...), custom_call_target="tpu_custom_call" | custom-call | tf_op jit(solution)/shard_map/pallas_call | solution.py:715
  74.7 1.9 %shard_map.154 = (bf16[128,1024]{1,0:T(8,128)(2,1)}, bf16[512,256]{1,0:T(8,128)(2,1)}, f32[3,16,256]{2,1,0:T(8,128)}, f32[16,256]{1,0:T(8,128)}, f32[16,256]{1,0...) custom-call(bf16[128,1024]{1,0:T(8,128)(2,1)} %get-tuple-element.21.refs_0_, ...), custom_call_target="tpu_custom_call" | custom-call | tf_op jit(solution)/shard_map/pallas_call | solution.py:728
